TPU v7x, 256 devices: a whole 4x4x8 slice. The times are simulated.
256 devices in a mesh: segment: 2 (over x_lo), tensor: 8 (over y, x_hi), particle: 16 (over z, core).
Axes of the slice: x: 4 (x_hi: 2, x_lo: 2; x = x_hi * 2 + x_lo), y: 4, z: 8, core: 2. Of those that a mesh axis runs over, the one named last changes fastest.
Arguments:
- step_states: bfloat16 [2, 4096, 8192], P('segment', 'particle', 'tensor'), may hold values from -1.5 to 1.5
- norm_gain: float32 [2, 1, 8192], P('segment'), may hold values from 0.1 to 1.9
- w_qkv: bfloat16 [2, 1, 8192, 6144], P('segment', None, 'particle', 'tensor'), may hold values from -0.0625 to 0.0625
- w_out: bfloat16 [2, 1, 8192, 4096], P('segment', None, 'particle', 'tensor'), may hold values from -0.09375 to 0.09375
- prefix_cache: bfloat16 [2, 1, 64, 2, 8, 256, 128], P('segment', None, 'particle', None, 'tensor'), may hold values from -3000 to 3000
- ancestors: int32 [2, 64], P('segment', 'particle'), may hold values from 0 to 63, as said below
- prefix_lengths: int32 [2, 64], P('segment'), may hold values from 32 to 256, as said below
Outputs:
- section_outputs: bfloat16 [2, 4096, 8192], P('segment', 'particle', 'tensor')
Inputs may be any that keep to these rules, and one draw needn't show every extreme that they name: `ancestors`: particles form blocks of 4 consecutive ones, 16 blocks on a cycle. A particle's ancestor lies in its own block, the one before or the one after. Every block has a particle descended from the block before and one descended from the block after; at most 3 of a block's particles descend from the block before, at most 3 from the block after, and both bounds are reached in every draw. `prefix_lengths`: in each section some particle's prefix fills all 256 cached positions.
All inputs are finite; a program needn't handle non-finite values.
Results may differ from a plain program's by a relative error of at most 0.015.
The roundings to bfloat16 on the way count: a program that leaves them out, or rounds other values in their place, can miss the bound.
Values may be sent and summed in bfloat16 or wider, within the bound.
No kernel may reach another device: no remote copies, remote signals or barrier semaphores. Data moves between devices by JAX's collectives and lax.ppermute only.
A program may use at most 128 MiB of HBM per device.

v0:
```python
import jax
import jax.numpy as jnp
from jax import lax
from jax.sharding import PartitionSpec as P

Q_HEADS = 32
KV_HEADS = 8


ROPE_BASE = 1000000.0
NORM_EPSILON = 1e-06


def extended_2(cells, sides, width):
    for axis, dim in sides:
        count = lax.axis_size(axis)
        head = lax.slice_in_dim(cells, 0, width, axis=dim)
        tail = lax.slice_in_dim(cells, cells.shape[dim] - width, cells.shape[dim], axis=dim)
        cells = jnp.concatenate(
            [
                lax.ppermute(tail, axis, [(i, (i + 1) % count) for i in range(count)]),
                cells,
                lax.ppermute(head, axis, [((i + 1) % count, i) for i in range(count)]),
            ],
            axis=dim,
        )
    return cells


def from_partner(value, axis, apart):
    mask = 2**apart
    pairs = [(source, source ^ mask) for source in range(lax.axis_size(axis))]
    return lax.ppermute(value, axis, pairs)


def rotate(values_in, positions):
    half_width = values_in.shape[-1] // 2
    frequency = ROPE_BASE ** (
        -(jnp.arange(half_width, dtype=jnp.float32) * 2.0 / values_in.shape[-1])
    )
    angles = positions.astype(jnp.float32)[..., None] * frequency
    cosine_part = jnp.cos(angles)
    sine_part = jnp.sin(angles)
    front_half = values_in[..., :half_width]
    back_half = values_in[..., half_width:]
    return jnp.concatenate(
        [
            front_half * cosine_part - back_half * sine_part,
            back_half * cosine_part + front_half * sine_part,
        ],
        -1,
    )


def attend(projected, cache, lengths, group_heads):
    particles = cache.shape[0]
    groups = cache.shape[2]
    prefix = cache.shape[3]
    head_size = cache.shape[4]
    step_tokens = projected.shape[0] // particles
    arranged = projected.reshape(particles, step_tokens, groups, group_heads + 2, head_size)
    positions = lengths[:, None] + jnp.arange(step_tokens, dtype=jnp.int32)[None, :]
    queries = rotate(arranged[:, :, :, :group_heads], positions[:, :, None, None]).astype(
        jnp.bfloat16
    )
    keys_new = rotate(arranged[:, :, :, group_heads], positions[:, :, None]).astype(jnp.bfloat16)
    values_new = arranged[:, :, :, group_heads + 1].astype(jnp.bfloat16)
    score_scale = 1.0 / jnp.sqrt(jnp.float32(head_size))
    cache_scores = (
        jnp.einsum("psgih,pglh->pgisl", queries, cache[:, 0], preferred_element_type=jnp.float32)
        * score_scale
    )
    visible = jnp.arange(prefix, dtype=jnp.int32)[None, :] < lengths[:, None]
    cache_scores = jnp.where(visible[:, None, None, None, :], cache_scores, -1e30)
    step_scores = (
        jnp.einsum("psgih,ptgh->pgist", queries, keys_new, preferred_element_type=jnp.float32)
        * score_scale
    )
    causal = jnp.arange(step_tokens)[:, None] >= jnp.arange(step_tokens)[None, :]
    step_scores = jnp.where(causal, step_scores, -1e30)
    peak = jnp.maximum(
        jnp.max(cache_scores, -1, keepdims=True), jnp.max(step_scores, -1, keepdims=True)
    )
    cache_weights = jnp.exp(cache_scores - peak)
    step_weights = jnp.exp(step_scores - peak)
    denominator = jnp.sum(cache_weights, -1, keepdims=True) + jnp.sum(
        step_weights, -1, keepdims=True
    )
    cache_probs = (cache_weights / denominator).astype(jnp.bfloat16)
    step_probs = (step_weights / denominator).astype(jnp.bfloat16)
    attended = jnp.einsum(
        "pgisl,pglh->psgih", cache_probs, cache[:, 1], preferred_element_type=jnp.float32
    )
    attended = attended + jnp.einsum(
        "pgist,ptgh->psgih", step_probs, values_new, preferred_element_type=jnp.float32
    )
    return attended.astype(jnp.bfloat16).reshape(
        particles * step_tokens, groups * group_heads * head_size
    )


def one_hot(chosen, columns):
    return (chosen[:, None] == jnp.arange(columns, dtype=jnp.int32)[None, :]).astype(jnp.bfloat16)


def pick_rows(selector, source):
    flattened = source.reshape(source.shape[0], source.shape[1], -1)
    selected = jnp.einsum("jk,lkr->ljr", selector, flattened, preferred_element_type=jnp.float32)
    return selected.astype(jnp.bfloat16).reshape(
        (source.shape[0], selector.shape[0]) + source.shape[2:]
    )


def body(step_states, norm_gain, w_qkv, w_out, prefix_cache, ancestors, prefix_lengths):
    devices = lax.axis_size("particle")
    own_index = lax.axis_index("particle")
    per_device = ancestors.shape[1]
    parents = ancestors[0]
    length_table = prefix_lengths[0]
    lengths = jnp.sum(
        jnp.where(
            parents[:, None] == jnp.arange(length_table.shape[0], dtype=jnp.int32)[None, :],
            length_table[None, :],
            0,
        ),
        axis=1,
    )
    distance = (parents // per_device - own_index) % devices
    offset = jnp.where(distance == 0, 0, jnp.where(distance == 1, 1, -1))
    source_row = parents % per_device
    caches = prefix_cache[0]
    extended = extended_2(caches, (("particle", 1),), per_device)
    picked = pick_rows(one_hot((offset + 1) * per_device + source_row, 3 * per_device), extended)
    group_heads = Q_HEADS // KV_HEADS
    hidden = step_states[0]
    whole = lax.all_gather(hidden, "tensor", axis=1, tiled=True)
    full_rows = whole.astype(jnp.float32)
    normed = (
        full_rows
        * lax.rsqrt(jnp.mean(full_rows * full_rows, -1, keepdims=True) + NORM_EPSILON)
        * norm_gain[0, 0]
    ).astype(jnp.bfloat16)
    projected = jnp.dot(
        normed,
        lax.all_gather(w_qkv[0, 0], "particle", axis=0, tiled=True),
        preferred_element_type=jnp.float32,
    )
    attended = attend(projected, picked[0], lengths, group_heads)
    partial_value = lax.dot_general(
        attended,
        lax.all_gather(w_out[0, 0], "particle", axis=0, tiled=True),
        (((1,), (1,)), ((), ())),
        preferred_element_type=jnp.float32,
    )
    summed = lax.psum_scatter(
        partial_value.astype(jnp.bfloat16), "tensor", scatter_dimension=1, tiled=True
    ).astype(jnp.float32)
    hidden = (hidden.astype(jnp.float32) + summed).astype(jnp.bfloat16)
    result = from_partner(hidden, "segment", 0)
    return result[None]


def solution(mesh):
    placed = (
        P("segment", "particle", "tensor"),
        P("segment", None, None),
        P("segment", None, "particle", "tensor"),
        P("segment", None, "particle", "tensor"),
        P("segment", None, "particle", None, "tensor", None, None),
        P("segment", "particle"),
        P("segment", None),
    )
    return jax.shard_map(
        body,
        mesh=mesh,
        in_specs=placed,
        out_specs=P("segment", "particle", "tensor"),
        check_vma=False,
    )
```

profile of v0, /device:TPU:32, one launch (start us, length us, event | category | flops | bytes accessed | tf_op | source)
XLA Modules:
  0.0 338.2 jit_solution(11371329569430238324)
XLA Ops:
  6.5 0.7 all-gather.7.cloned.1.call-update
  7.3 0.7 all-gather.9.cloned.1.call-update
  8.1 0.7 all-gather.11.cloned.1.call-update
  8.8 1.7 collective-permute-start.1
  10.5 1.3 concatenate.34
  11.8 0.9 select_reduce_fusion
  12.7 0.7 fusion.48
  13.5 0.5 multiply_cosine_fusion.1
  14.1 3.5 %collective-permute-done = bf16[1,4,2,1,256,128]{5,4,2,1,3,0:T(8,128)(2,1)S(1)} collective-permute-done((bf16[1,4,2,1,256,128]{5,4,2,1,3,0:T(8,128)(2,1)}, bf16[1,4,2,1,256,128]{5,4,2,1,3,0:T(8,128)(2,1)S(1)}, u32[]{:S(2)}, u32[]{:S(2)}) %collective-permute-start) | collective-permute-done | bytes 524320 | tf_op jit(solution)/shard_map/ppermute | solution.py:21
  17.6 0.2 concatenate.33
  17.8 0.2 concatenate.35
  18.0 1.1 fusion.17
  19.2 69.9 %all-gather.7.cloned.1.call-done = bf16[1,256,8192]{2,1,0:T(8,128)(2,1)} async-done(((bf16[1,256,1024]{2,1,0:T(8,128)(2,1)}), bf16[1,256,8192]{2,1,0:T(8,128)(2,1)}) %all-gather.7.cloned.1.call-update) | async-done | bytes 4194320 | tf_op jit(solution)/shard_map/all_gather | solution.py:136
  89.0 3.1 fusion.2
  92.2 70.5 %all-gather.9.cloned.1.call-done = bf16[1,1,8192,768]{3,2,1,0:T(8,128)(2,1)} async-done(((bf16[1,1,512,768]{3,2,1,0:T(8,128)(2,1)}), bf16[1,1,8192,768]{3,2,1,0:T(8,128)(2,1)}) %all-gather.9.cloned.1.call-update) | async-done | bytes 12582928 | tf_op jit(solution)/shard_map/all_gather | solution.py:145
  162.6 9.0 %fusion = f32[256,768]{1,0:T(8,128)S(1)} fusion(bf16[1,1,8192,768]{3,2,1,0:T(8,128)(2,1)} %all-gather.9.cloned.1.call-done, bf16[1,256,8192]{2,1,0:T(8,128)(2,1)} %all-gather.7.cloned.1.call-done, f32[8192]{0:T(1024)S(1)} %bitcast.128, f32[256]{0:T(256)S(1)} %add_rsqrt_fusion), kind=kOutput, calls=%fused_computation.1 | convolution fusion | flops 3229614080 | bytes 17597440 | tf_op jit(solution)/shard_map/dot_general | solution.py:143
  172.1 0.6 fusion.46
  172.7 0.3 fusion.55
  173.0 0.2 fusion.27
  173.2 0.5 fusion.57
  173.7 0.5 fusion.56
  174.3 0.4 fusion.23
  174.7 0.7 fusion.24
  175.4 0.3 fusion.21
  175.7 0.2 copy.30
  175.9 43.1 %all-gather.11.cloned.1.call-done = bf16[1,1,8192,512]{3,2,1,0:T(8,128)(2,1)} async-done(((bf16[1,1,512,512]{3,2,1,0:T(8,128)(2,1)}), bf16[1,1,8192,512]{3,2,1,0:T(8,128)(2,1)}) %all-gather.11.cloned.1.call-update) | async-done | bytes 8388624 | tf_op jit(solution)/shard_map/all_gather | solution.py:151
  219.0 7.7 %convolution_convert_fusion.1 = bf16[256,8192]{1,0:T(8,128)(2,1)} fusion(bf16[1,1,8192,512]{3,2,1,0:T(8,128)(2,1)} %all-gather.11.cloned.1.call-done, bf16[32,8,4,128]{3,2,1,0:T(4,128)(2,1)S(1)} %bitcast.124), kind=kOutput, calls=%fused_computation.5 | convolution fusion | flops 2149580800 | bytes 12845056 | tf_op jit(solution)/shard_map/dot_general | solution.py:149
  226.7 90.1 %reduce-scatter.2.cloned.1.call-done = bf16[256,1024]{1,0:T(8,128)(2,1)} async-done(((bf16[256,8192]{1,0:T(8,128)(2,1)}), bf16[256,1024]{1,0:T(8,128)(2,1)}) %reduce-scatter.2.cloned.1.call-update) | async-done | bytes 524304 | tf_op jit(solution)/shard_map/reduce_scatter | solution.py:155
  316.9 1.2 fusion.22
  318.1 0.7 collective-permute-start.2
  318.8 12.1 %collective-permute-done.2 = bf16[256,1024]{1,0:T(8,128)(2,1)S(1)} collective-permute-done((bf16[256,1024]{1,0:T(8,128)(2,1)S(1)}, bf16[256,1024]{1,0:T(8,128)(2,1)S(1)}, u32[]{:S(2)}, u32[]{:S(2)}) %collective-permute-start.2) | collective-permute-done | bytes 524320 | tf_op jit(solution)/shard_map/ppermute | solution.py:33
  330.9 0.8 copy.67
  (24 shorter events, 0.9 us)
Async XLA Ops:
  6.5 82.5 %all-gather.7.cloned.1.call-start = ((), (), s32[]{:S(2)}) async-start(), calls=%async_computation.2 | async-start | bytes 4718592 | tf_op jit(solution)/shard_map/all_gather | solution.py:136
  7.3 155.4 %all-gather.9.cloned.1.call-start = ((), (), s32[]{:S(2)}) async-start(), calls=%async_computation.3 | async-start | bytes 13369344 | tf_op jit(solution)/shard_map/all_gather | solution.py:145
  8.0 211.0 %all-gather.11.cloned.1.call-start = ((), (), s32[]{:S(2)}) async-start(), calls=%async_computation.4 | async-start | bytes 8912896 | tf_op jit(solution)/shard_map/all_gather | solution.py:151
  8.7 308.1 %reduce-scatter.2.cloned.1.call-start = ((), (), s32[]{:S(2)}) async-start(), calls=%async_computation.1 | async-start | bytes 4718592 | tf_op jit(solution)/shard_map/reduce_scatter | solution.py:155
  8.8 8.8 %collective-permute-start = (bf16[1,4,2,1,256,128]{5,4,2,1,3,0:T(8,128)(2,1)}, bf16[1,4,2,1,256,128]{5,4,2,1,3,0:T(8,128)(2,1)S(1)}, u32[]{:S(2)}, u32[]{:S(2)}) collective-permute-start(bf16[1,4,2,1,256,128]{5,4,2,1,3,0:T(8,128)(2,1)} %bitcast.125), channel_id=1, source_target_pairs={{0,1},{1,2},{2,3},{3,4},{4,5},{5,6},{6,7},{7,8},{8,9},{9,10},{10,1... | collective-permute-start | bytes 1572872 | tf_op jit(solution)/shard_map/ppermute | solution.py:21
  8.8 9.0 %collective-permute-start.1 = (bf16[1,4,2,1,256,128]{5,4,2,1,3,0:T(8,128)(2,1)}, bf16[1,4,2,1,256,128]{5,4,2,1,3,0:T(8,128)(2,1)S(1)}, u32[]{:S(2)}, u32[]{:S(2)}) collective-permute-start(bf16[1,4,2,1,256,128]{5,4,2,1,3,0:T(8,128)(2,1)} %bitcast.126), channel_id=1, source_target_pairs={{1,0},{2,1},{3,2},{4,3},{5,4},{6,5},{7,6},{8,7},{9,8},{10,9},{11,1... | collective-permute-start | bytes 1572872 | tf_op jit(solution)/shard_map/ppermute | solution.py:23
  18.0 144.6 %copy-start.1 = (f32[1,1,8192]{2,1,0:T(1,128)S(1)}, f32[1,1,8192]{2,1,0:T(1,128)}, u32[]{:S(2)}) copy-start(f32[1,1,8192]{2,1,0:T(1,128)} %param.8) | copy-start | bytes 98308
  226.7 90.2 %copy-start = (bf16[1,256,1024]{2,1,0:T(8,128)(2,1)S(1)}, bf16[1,256,1024]{2,1,0:T(8,128)(2,1)}, u32[]{:S(2)}) copy-start(bf16[1,256,1024]{2,1,0:T(8,128)(2,1)} %param.7) | copy-start | bytes 1572868
  318.1 12.8 %collective-permute-start.2 = (bf16[256,1024]{1,0:T(8,128)(2,1)S(1)}, bf16[256,1024]{1,0:T(8,128)(2,1)S(1)}, u32[]{:S(2)}, u32[]{:S(2)}) collective-permute-start(bf16[256,1024]{1,0:T(8,128)(2,1)S(1)} %fusion.22), channel_id=1, source_target_pairs={{0,128},{128,0},{1,129},{129,1},{2,130},{130,2},{3,131},{131,3},{4... | collective-permute-start | bytes 1572872 | tf_op jit(solution)/shard_map/ppermute | solution.py:33
Sparse Core Ops, SparseCore 0:
  10.0 79.0 all-gather.6
  90.9 71.6 all-gather.8
  164.5 54.4 all-gather.10
  226.8 89.9 reduce-scatter.1
where the time goes:
time: 338 us
  waiting for transfers between devices  291 us (86%)
  matrix products  19.7 us (6%)
  between operations  13.3 us (4%)
  other arithmetic  7.84 us (2%)
  local copies, waits for them, and re-layouts  3.46 us (1%)
    reduce_scatter x1, waiting for transfers between devices, body(): lax.psum_scatter(partial_value.astype(jnp.bfloat16), 'tensor', scatter_di...  90.1 us
    all_gather x1, waiting for transfers between devices, body(): lax.all_gather(w_qkv[0, 0], 'particle', axis=0, tiled=True)  70.5 us
    all_gather x1, waiting for transfers between devices, body(): whole = lax.all_gather(hidden, 'tensor', axis=1, tiled=True)  69.9 us
    all_gather x1, waiting for transfers between devices, body(): lax.all_gather(w_out[0, 0], 'particle', axis=0, tiled=True)  43.1 us
    ppermute x1, waiting for transfers between devices, from_partner(): return lax.ppermute(value, axis, pairs)  12.1 us
    dot_general x1, matrix products, body(): jnp.dot(normed, lax.all_gather(w_qkv[0, 0], 'particle', axis=0, tiled=Tru...  9.03 us
    dot_general x1, matrix products, body(): lax.dot_general(attended, lax.all_gather(w_out[0, 0], 'particle', axis=0,...  7.69 us
  transfers between devices with their start and end apart: 7, of which 6 were waited for; matrix products, arithmetic and copies ran while one was open for 6% of the time, Pallas kernels for 0%

commit v1 on v0

v1 whole, which is shorter than its diff:
```python
import jax
import jax.numpy as jnp
from jax import lax
from jax.experimental import pallas as pl
from jax.experimental.pallas import tpu as pltpu
from jax.sharding import PartitionSpec as P

Q_HEADS = 32
KV_HEADS = 8

ROPE_BASE = 1000000.0
NORM_EPSILON = 1e-06

AXES = ("segment", "tensor", "particle")
SEG, NY, NXH, NZ, NC = 2, 4, 2, 8, 2
SCOPE = pltpu.CompilerParams(vmem_limit_bytes=40 * 2**20)


def moves(ds=0, dy=0, dxh=0, dz=0, dc=0):
    pairs = []
    for s in range(SEG):
        for y in range(NY):
            for xh in range(NXH):
                for z in range(NZ):
                    for c in range(NC):
                        src = ((s * NY + y) * NXH + xh) * NZ * NC + z * NC + c
                        to = (
                            ((s + ds) % SEG * NY + (y + dy) % NY) * NXH + (xh + dxh) % NXH
                        ) * NZ * NC + (z + dz) % NZ * NC + (c + dc) % NC
                        pairs.append((src, to))
    return pairs


def send(value, **shift):
    return lax.ppermute(value, AXES, moves(**shift))


def rotation(lengths, step_tokens, head_size):
    half_width = head_size // 2
    frequency = ROPE_BASE ** (
        -(jnp.arange(half_width, dtype=jnp.float32) * 2.0 / head_size)
    )
    positions = lengths[:, None] + jnp.arange(step_tokens, dtype=jnp.int32)[None, :]
    angles = positions.reshape(-1).astype(jnp.float32)[:, None] * frequency
    cosine_part = jnp.cos(angles)
    sine_part = jnp.sin(angles)
    return (
        jnp.concatenate([cosine_part, cosine_part], axis=1),
        jnp.concatenate([-sine_part, sine_part], axis=1),
    )


def attend_kernel(group_heads, lengths_ref, x_ref, cos_ref, sin_ref, cache_ref, o_ref):
    particles, _, prefix, head = cache_ref.shape
    steps = x_ref.shape[0] // particles
    score_scale = 1.0 / jnp.sqrt(jnp.float32(head))
    across = (((1,), (1,)), ((), ()))
    for p in range(particles):
        mine = pl.ds(p * steps, steps)
        cosine_part, sine_part = cos_ref[mine, :], sin_ref[mine, :]

        def rotated(k):
            v = x_ref[mine, k * head : (k + 1) * head]
            return v * cosine_part + pltpu.roll(v, head // 2, 1) * sine_part

        queries = jnp.concatenate([rotated(k) for k in range(group_heads)], axis=0)
        queries = queries.astype(jnp.bfloat16)
        keys_new = rotated(group_heads).astype(jnp.bfloat16)
        values_new = x_ref[mine, (group_heads + 1) * head :].astype(jnp.bfloat16)
        cache_scores = (
            lax.dot_general(queries, cache_ref[p, 0], across, preferred_element_type=jnp.float32)
            * score_scale
        )
        spots = lax.broadcasted_iota(jnp.int32, cache_scores.shape, 1)
        cache_scores = jnp.where(spots < lengths_ref[p], cache_scores, -1e30)
        step_scores = (
            lax.dot_general(queries, keys_new, across, preferred_element_type=jnp.float32)
            * score_scale
        )
        token = lax.rem(lax.broadcasted_iota(jnp.int32, step_scores.shape, 0), steps)
        other = lax.broadcasted_iota(jnp.int32, step_scores.shape, 1)
        step_scores = jnp.where(token >= other, step_scores, -1e30)
        peak = jnp.maximum(
            jnp.max(cache_scores, -1, keepdims=True), jnp.max(step_scores, -1, keepdims=True)
        )
        cache_weights = jnp.exp(cache_scores - peak)
        step_weights = jnp.exp(step_scores - peak)
        share = 1.0 / (
            jnp.sum(cache_weights, -1, keepdims=True) + jnp.sum(step_weights, -1, keepdims=True)
        )
        attended = jnp.dot(
            (cache_weights * share).astype(jnp.bfloat16),
            cache_ref[p, 1],
            preferred_element_type=jnp.float32,
        ) + jnp.dot(
            (step_weights * share).astype(jnp.bfloat16),
            values_new,
            preferred_element_type=jnp.float32,
        )
        attended = attended.astype(jnp.bfloat16)
        for k in range(group_heads):
            o_ref[mine, k * head : (k + 1) * head] = attended[k * steps : (k + 1) * steps]


def attend(projected, cosine_part, sine_part, cache, lengths, group_heads):
    head = cache.shape[-1]
    whole = pl.BlockSpec(memory_space=pltpu.VMEM)
    return pl.pallas_call(
        lambda *refs: attend_kernel(group_heads, *refs),
        in_specs=[pl.BlockSpec(memory_space=pltpu.SMEM)] + [whole] * 4,
        out_specs=whole,
        out_shape=jax.ShapeDtypeStruct((projected.shape[0], group_heads * head), jnp.bfloat16),
        compiler_params=SCOPE,
        cost_estimate=pl.CostEstimate(
            flops=4 * projected.shape[0] * group_heads * head * (cache.shape[2] + 64),
            bytes_accessed=2 * cache.size + 4 * projected.size,
            transcendentals=0,
        ),
    )(lengths, projected, cosine_part, sine_part, cache)


def one_hot(chosen, columns):
    return (chosen[:, None] == jnp.arange(columns, dtype=jnp.int32)[None, :]).astype(jnp.bfloat16)


def pick_rows(selector, source):
    flattened = source.reshape(source.shape[0], source.shape[1], -1)
    selected = jnp.einsum("jk,lkr->ljr", selector, flattened, preferred_element_type=jnp.float32)
    return selected.astype(jnp.bfloat16).reshape(
        (source.shape[0], selector.shape[0]) + source.shape[2:]
    )


def picked_cache(prefix_cache, ancestors, prefix_lengths):
    devices = lax.axis_size("particle")
    own_index = lax.axis_index("particle")
    per_device = ancestors.shape[1]
    parents = ancestors[0]
    length_table = prefix_lengths[0]
    lengths = jnp.sum(
        jnp.where(
            parents[:, None] == jnp.arange(length_table.shape[0], dtype=jnp.int32)[None, :],
            length_table[None, :],
            0,
        ),
        axis=1,
    )
    distance = (parents // per_device - own_index) % devices
    offset = jnp.where(distance == 0, 0, jnp.where(distance == 1, 1, -1))
    source_row = parents % per_device
    caches = prefix_cache[0]
    before = lax.ppermute(caches, "particle", [(i, (i + 1) % devices) for i in range(devices)])
    after = lax.ppermute(caches, "particle", [((i + 1) % devices, i) for i in range(devices)])
    extended = jnp.concatenate([before, caches, after], axis=1)
    picked = pick_rows(one_hot((offset + 1) * per_device + source_row, 3 * per_device), extended)
    return picked[0], lengths


def ring(block):
    half = block.shape[0] // 2
    found = {0: block}
    flow = {1: block, -1: block}
    for step in range(1, NZ // 2):
        for d in (1, -1):
            flow[d] = send(flow[d], dz=d)
            found[-d * step % NZ] = flow[d]
    far_low = send(flow[1][:half], dz=1)
    far_high = send(flow[-1][half:], dz=-1)
    found[NZ // 2] = jnp.concatenate([far_low, far_high], axis=0)
    return found


def term(a, w):
    return lax.dot_general(
        a, w, (((1,), (1,)), ((), ())), preferred_element_type=jnp.float32
    ).astype(jnp.bfloat16)


def terms_kernel(a_ref, w_ref, o_ref):
    o_ref[0] = term(a_ref[...], w_ref[...])


def head_terms(a, w):
    shards = NY * NXH
    rows = w.shape[0] // shards
    return pl.pallas_call(
        terms_kernel,
        grid=(shards,),
        in_specs=[
            pl.BlockSpec(a.shape, lambda k: (0, 0)),
            pl.BlockSpec((rows, w.shape[1]), lambda k: (k, 0)),
        ],
        out_specs=pl.BlockSpec((1, a.shape[0], rows), lambda k: (k, 0, 0)),
        out_shape=jax.ShapeDtypeStruct((shards, a.shape[0], rows), jnp.bfloat16),
        compiler_params=SCOPE,
        cost_estimate=pl.CostEstimate(
            flops=2 * a.size * w.shape[0],
            bytes_accessed=2 * (a.size + w.size + a.shape[0] * w.shape[0]),
            transcendentals=0,
        ),
    )(a, w)


def ring_terms_kernel(order, place_ref, a_ref, *refs):
    own, partners, o_ref = refs[: len(order)], refs[len(order) : -1], refs[-1]
    z, c = place_ref[0], place_ref[1]
    rows = own[0].shape[0]
    a = a_ref[...]
    at = 0
    for k, block in zip(order, own):
        to = lax.rem(z + k, NZ)
        o_ref[to, :, pl.ds(pl.multiple_of(c * rows, rows), rows)] = term(a, block[...])
    for group in partners:
        for g in range(group.shape[0]):
            to = lax.rem(z + order[at], NZ)
            o_ref[to, :, pl.ds(pl.multiple_of((1 - c) * rows, rows), rows)] = term(a, group[g])
            at += 1


def ring_terms(a, order, own, partners, place):
    rows = own[0].shape[0]
    whole = pl.BlockSpec(memory_space=pltpu.VMEM)
    return pl.pallas_call(
        lambda *refs: ring_terms_kernel(order, *refs),
        in_specs=[pl.BlockSpec(memory_space=pltpu.SMEM)]
        + [whole] * (1 + len(own) + len(partners)),
        out_specs=whole,
        out_shape=jax.ShapeDtypeStruct((NZ, a.shape[0], NC * rows), jnp.bfloat16),
        compiler_params=SCOPE,
        cost_estimate=pl.CostEstimate(
            flops=2 * a.size * NZ * NC * rows,
            bytes_accessed=2 * (a.size + NZ * NC * rows * (a.shape[0] + a.shape[1])),
            transcendentals=0,
        ),
    )(place, a, *own, *partners)


def body(step_states, norm_gain, w_qkv, w_out, prefix_cache, ancestors, prefix_lengths):
    t = lax.axis_index("tensor")
    y, xh = t // NXH, t % NXH
    z, c = lax.axis_index("particle") // NC, lax.axis_index("particle") % NC
    group_heads = Q_HEADS // KV_HEADS
    x0 = step_states[0]
    tokens, features = x0.shape
    shards = NY * NXH
    rows = w_out.shape[2] // 2

    w_full = lax.all_gather(w_qkv[0, 0], "particle", axis=0, tiled=True)

    pair = jnp.stack([x0, send(x0, dxh=1)])
    from_before = send(pair, dy=1)
    from_after = send(pair, dy=-1)
    far_a = send(from_before[0], dy=1)
    far_b = send(from_after[1], dy=-1)
    found = jnp.concatenate([pair, from_after, jnp.stack([far_a, far_b]), from_before], axis=0)
    blocks = [
        lax.dynamic_index_in_dim(
            found, ((k // NXH - y) % NY) * NXH + (k + xh) % NXH, axis=0, keepdims=False
        )
        for k in range(shards)
    ]
    full_rows = jnp.concatenate(blocks, axis=1).astype(jnp.float32)
    normed = (
        full_rows
        * lax.rsqrt(jnp.mean(full_rows * full_rows, -1, keepdims=True) + NORM_EPSILON)
        * norm_gain[0, 0]
    ).astype(jnp.bfloat16)

    hidden = send(x0, ds=1)
    picked, lengths = picked_cache(prefix_cache, ancestors, prefix_lengths)

    around = ring(w_out[0, 0, :rows])
    order = (0, 1, 7, 2, 6, 3, 5, 4)
    own = [around[k] for k in order]
    partners = [send(jnp.stack(own[:5]), dc=1), send(jnp.stack(own[5:]), dc=1)]

    cosine_part, sine_part = rotation(lengths, tokens // ancestors.shape[1], picked.shape[-1])
    cache = picked.reshape(picked.shape[0], 2, picked.shape[3], picked.shape[4])
    w_full, normed, cache, cosine_part, sine_part, hidden, own, partners = lax.optimization_barrier(
        (w_full, normed, cache, cosine_part, sine_part, hidden, own, partners)
    )
    second = lax.all_gather(w_out[0, 0, rows:], "particle", axis=0, tiled=True)
    projected = jnp.dot(normed, w_full, preferred_element_type=jnp.float32)
    attended = attend(projected, cosine_part, sine_part, cache, lengths, group_heads)

    results = []
    for half in range(2):
        if half == 0:
            terms = ring_terms(attended, order, own, partners, jnp.stack([z, c]))
        else:
            terms = head_terms(attended, second)
        terms = terms.reshape(NY, NXH, tokens, NC * rows)
        mid = tokens // 2

        def low_high(dy):
            block = lax.dynamic_index_in_dim(terms, (y + dy) % NY, axis=0, keepdims=False)
            return block[:, :mid], block[:, mid:]

        far_up, far_down = low_high(2)
        far_up, far_down = send(far_up, dy=1), send(far_down, dy=-1)
        up_low, up_high = low_high(1)
        down_low, down_high = low_high(-1)
        direct_up, direct_down = send(up_high, dy=1), send(down_low, dy=-1)
        relayed_up = send(
            (up_low.astype(jnp.float32) + far_up.astype(jnp.float32)).astype(jnp.bfloat16), dy=1
        )
        relayed_down = send(
            (down_high.astype(jnp.float32) + far_down.astype(jnp.float32)).astype(jnp.bfloat16),
            dy=-1,
        )
        here_low, here_high = low_high(0)
        low = (
            here_low.astype(jnp.float32)
            + relayed_up.astype(jnp.float32)
            + direct_down.astype(jnp.float32)
        )
        high = (
            here_high.astype(jnp.float32)
            + relayed_down.astype(jnp.float32)
            + direct_up.astype(jnp.float32)
        )
        summed = jnp.concatenate([low, high], axis=1).astype(jnp.bfloat16)
        attended, summed = lax.optimization_barrier((attended, summed))
        same = send(jnp.where(xh == 0, summed[0], summed[1]), ds=1)
        cross = send(jnp.where(xh == 0, summed[1], summed[0]), ds=1, dxh=1)
        results.append(same.astype(jnp.float32) + cross.astype(jnp.float32))
    summed = jnp.concatenate(
        [r[:, k * rows : (k + 1) * rows] for k in range(NC) for r in results], axis=1
    )
    return (hidden.astype(jnp.float32) + summed).astype(jnp.bfloat16)[None]


def solution(mesh):
    placed = (
        P("segment", "particle", "tensor"),
        P("segment", None, None),
        P("segment", None, "particle", "tensor"),
        P("segment", None, "particle", "tensor"),
        P("segment", None, "particle", None, "tensor", None, None),
        P("segment", "particle"),
        P("segment", None),
    )
    return jax.shard_map(
        body,
        mesh=mesh,
        in_specs=placed,
        out_specs=P("segment", "particle", "tensor"),
        check_vma=False,
    )
```

time: 338 us -> 194 us (0.57)
  waiting for transfers between devices: 291 us -> 76.7 us
  starting transfers between devices: 2.53 us -> 53.3 us
  local copies, waits for them, and re-layouts: 3.46 us -> 18.3 us
  matrix products: 19.7 us -> 11.2 us
  Pallas kernels: 0 us -> 7.01 us
  other arithmetic: 7.84 us -> 12.4 us
    all_gather x3 -> x2, waiting for transfers between devices: 183 us -> 20.2 us  [the longest x1 11.9 us: body(): w_full = lax.all_gather(w_qkv[0, 0], 'particle', axis=0, tiled=True)]
    reduce_scatter x1 -> x0, waiting for transfers between devices: 90.1 us -> none  [body(): lax.psum_scatter(partial_value.astype(jnp.bfloat16), 'tensor', scatter_di...]
    ppermute x3 -> x34, starting transfers between devices: 2.42 us -> 53.2 us  [the longest x32 50.1 us: send(): return lax.ppermute(value, AXES, moves(**shift))]
    ppermute x3 -> x34, waiting for transfers between devices: 15.7 us -> 55.7 us  [the longest x32 55.7 us: send(): return lax.ppermute(value, AXES, moves(**shift))]
    dot_general x6 -> x1, matrix products: 18.6 us -> 8.95 us  [body(): projected = jnp.dot(normed, w_full, preferred_element_type=jnp.float32)]
    unnamed x7 -> x48, local copies, waits for them, and re-layouts: 0.88 us -> 10 us
    pallas_call x0 -> x3, Pallas kernels: none -> 7.01 us  [the longest x1 2.73 us: head_terms(): pl.pallas_call(terms_kernel, grid=(shards,), in_specs=[pl.BlockSpec(a.sha...]
  transfers between devices with their start and end apart: 7 -> 36, of which waited for: 6 -> 20; matrix products, arithmetic and copies ran while one was open for 6% -> 19% of each run, Pallas kernels for 0% -> 2%
where the time goes in v1:
time: 194 us; the launch traced here: 193 us
  waiting for transfers between devices  76.7 us (40%)
  starting transfers between devices  53.3 us (27%)
  local copies, waits for them, and re-layouts  18.3 us (9%)
  between operations  14.1 us (7%)
  other arithmetic  12.4 us (6%)
  matrix products  11.2 us (6%)
  Pallas kernels  7.01 us (4%)
    ppermute x32, waiting for transfers between devices, send(): return lax.ppermute(value, AXES, moves(**shift))  55.7 us
    ppermute x32, starting transfers between devices, send(): return lax.ppermute(value, AXES, moves(**shift))  50.1 us
    all_gather x1, waiting for transfers between devices, body(): w_full = lax.all_gather(w_qkv[0, 0], 'particle', axis=0, tiled=True)  11.9 us
    unnamed x48, local copies, waits for them, and re-layouts  10 us
    dot_general x1, matrix products, body(): projected = jnp.dot(normed, w_full, preferred_element_type=jnp.float32)  8.95 us
    all_gather x1, waiting for transfers between devices, body(): second = lax.all_gather(w_out[0, 0, rows:], 'particle', axis=0, tiled=True)  8.33 us
  transfers between devices with their start and end apart: 36, of which 20 were waited for; matrix products, arithmetic and copies ran while one was open for 19% of the time, Pallas kernels for 2%

profile of v1, /device:TPU:32, one launch (start us, length us, event | category | flops | bytes accessed | tf_op | source)
XLA Modules:
  0.0 192.8 jit_solution(16600767543645193428)
XLA Ops:
  11.1 3.1 %collective-permute-start.6 = (bf16[1,4,2,1,256,128]{5,4,2,1,3,0:T(8,128)(2,1)}, bf16[1,4,2,1,256,128]{5,4,2,1,3,0:T(8,128)(2,1)S(1)}, u32[]{:S(2)}, u32[]{:S(2)}) collective-permute-start(bf16[1,4,2,1,256,128]{5,4,2,1,3,0:T(8,128)(2,1)} %bitcast.113), channel_id=1, source_target_pairs={{1,0},{2,1},{3,2},{4,3},{5,4},{6,5},{7,6},{8,7},{9,8},{10,9},{11,1... | collective-permute-start | bytes 1572872 | tf_op jit(solution)/shard_map/ppermute | solution.py:153
  14.2 3.0 %collective-permute-start = (bf16[256,1024]{1,0:T(8,128)(2,1)}, bf16[256,1024]{1,0:T(8,128)(2,1)S(1)}, u32[]{:S(2)}, u32[]{:S(2)}) collective-permute-start(bf16[256,1024]{1,0:T(8,128)(2,1)} %bitcast.1), channel_id=1, source_target_pairs={{0,16},{1,17},{2,18},{3,19},{4,20},{5,21},{6,22},{7,23},{8,24},{9,... | collective-permute-start | bytes 1572872 | tf_op jit(solution)/shard_map/ppermute | solution.py:35
  27.7 2.6 %collective-permute-done = bf16[256,1024]{1,0:T(8,128)(2,1)S(1)} collective-permute-done((bf16[256,1024]{1,0:T(8,128)(2,1)}, bf16[256,1024]{1,0:T(8,128)(2,1)S(1)}, u32[]{:S(2)}, u32[]{:S(2)}) %collective-permute-start) | collective-permute-done | bytes 524320 | tf_op jit(solution)/shard_map/ppermute | solution.py:35
  30.2 3.1 %collective-permute-start.10 = (bf16[256,512]{1,0:T(8,128)(2,1)S(1)}, bf16[256,512]{1,0:T(8,128)(2,1)S(1)}, u32[]{:S(2)}, u32[]{:S(2)}) collective-permute-start(bf16[256,512]{1,0:T(8,128)(2,1)S(1)} %collective-permute-done.8.refs_3_), channel_id=1, source_target_pairs={{0,14},{1,15},{2,0},{3,1},{4,2},{5,3},{6,4},{7,5},{8,6},{9,7},{10,... | collective-permute-start | bytes 786440 | tf_op jit(solution)/shard_map/ppermute | solution.py:35
  35.5 3.0 %collective-permute-start.1 = (bf16[2,256,1024]{2,1,0:T(8,128)(2,1)}, bf16[2,256,1024]{2,1,0:T(8,128)(2,1)}, u32[]{:S(2)}, u32[]{:S(2)}) collective-permute-start(bf16[2,256,1024]{2,1,0:T(8,128)(2,1)} %pad_maximum_fusion), channel_id=1, source_target_pairs={{0,96},{1,97},{2,98},{3,99},{4,100},{5,101},{6,102},{7,103},{8,104... | collective-permute-start | bytes 3145736 | tf_op jit(solution)/shard_map/ppermute | solution.py:35
  39.7 2.3 %fusion.7 = bf16[1,4,512,128]{3,1,2,0:T(4,128)(2,1)S(1)} fusion(bf16[1,4,65536]{2,1,0:T(4,128)(2,1)S(1)} %concatenate.41, bf16[1,4,65536]{2,1,0:T(4,128)(2,1)S(1)} %copy-done.12, bf16[1,4,65536]{2,1,0:T(4,128)(2,1)} %concatenate.39, s32[4]{0:T(128)S(1)} %fusion.12), kind=kOutput, calls=%fused_computation.11 | convolution fusion | flops 11272240 | bytes 2097168 | tf_op jit(solution)/shard_map/jk,lkr->ljr/dot_general | solution.py:128
  42.2 2.4 %collective-permute-done.10.refs_5_ = bf16[256,512]{1,0:T(8,128)(2,1)S(1)} collective-permute-done((bf16[256,512]{1,0:T(8,128)(2,1)S(1)}, bf16[256,512]{1,0:T(8,128)(2,1)S(1)}, u32[]{:S(2)}, u32[]{:S(2)}) %collective-permute-start.10) | collective-permute-done | bytes 262176 | tf_op jit(solution)/shard_map/ppermute | solution.py:35
  46.5 9.0 %collective-permute-done.13.refs_8_ = bf16[256,512]{1,0:T(8,128)(2,1)S(1)} collective-permute-done((bf16[256,512]{1,0:T(8,128)(2,1)S(1)}, bf16[256,512]{1,0:T(8,128)(2,1)S(1)}, u32[]{:S(2)}, u32[]{:S(2)}) %collective-permute-start.13) | collective-permute-done | bytes 262176 | tf_op jit(solution)/shard_map/ppermute | solution.py:35
  56.6 3.1 %collective-permute-done.12.refs_7_ = bf16[256,512]{1,0:T(8,128)(2,1)S(1)} collective-permute-done((bf16[256,512]{1,0:T(8,128)(2,1)S(1)}, bf16[256,512]{1,0:T(8,128)(2,1)S(1)}, u32[]{:S(2)}, u32[]{:S(2)}) %collective-permute-start.12) | collective-permute-done | bytes 262176 | tf_op jit(solution)/shard_map/ppermute | solution.py:35
  59.8 4.8 %collective-permute-done.14 = bf16[128,512]{1,0:T(8,128)(2,1)S(1)} collective-permute-done((bf16[128,512]{1,0:T(8,128)(2,1)S(1)}, bf16[128,512]{1,0:T(8,128)(2,1)S(1)}, u32[]{:S(2)}, u32[]{:S(2)}) %collective-permute-start.14) | collective-permute-done | bytes 131104 | tf_op jit(solution)/shard_map/ppermute | solution.py:35
  64.6 3.2 %collective-permute-start.15 = (bf16[128,512]{1,0:T(8,128)(2,1)S(1)}, bf16[128,512]{1,0:T(8,128)(2,1)S(1)}, u32[]{:S(2)}, u32[]{:S(2)}) collective-permute-start(bf16[128,512]{1,0:T(8,128)(2,1)S(1)} %slice.127), channel_id=1, source_target_pairs={{0,14},{1,15},{2,0},{3,1},{4,2},{5,3},{6,4},{7,5},{8,6},{9,7},{10,... | collective-permute-start | bytes 393224 | tf_op jit(solution)/shard_map/ppermute | solution.py:35
  75.0 4.4 %collective-permute-done.3 = bf16[256,1024]{1,0:T(8,128)(2,1)S(1)} collective-permute-done((bf16[256,1024]{1,0:T(8,128)(2,1)S(1)}, bf16[256,1024]{1,0:T(8,128)(2,1)S(1)}, u32[]{:S(2)}, u32[]{:S(2)}) %collective-permute-start.3) | collective-permute-done | bytes 524320 | tf_op jit(solution)/shard_map/ppermute | solution.py:35
  83.7 3.2 %fusion.2 = bf16[256,8192]{1,0:T(8,128)(2,1)} fusion(bf16[256,8192]{1,0:T(8,128)(2,1)S(1)} %bitcast_dynamic-update-slice_fusion, f32[8192]{0:T(1024)S(1)} %bitcast.114, f32[256]{0:T(256)S(1)} %add_rsqrt_fusion), kind=kLoop, calls=%fused_computation.5 | loop fusion | flops 8388608 | bytes 8422400 | tf_op jit(solution)/shard_map/convert_element_type | solution.py:267
  87.8 11.9 %all-gather.5.cloned.1.call-done = bf16[1,1,8192,768]{3,2,1,0:T(8,128)(2,1)} async-done(((bf16[1,1,512,768]{3,2,1,0:T(8,128)(2,1)}), bf16[1,1,8192,768]{3,2,1,0:T(8,128)(2,1)}) %all-gather.5.cloned.1.call-update) | async-done | bytes 12582928 | tf_op jit(solution)/shard_map/all_gather | solution.py:248
  99.7 9.0 %fusion.22.refs_1_ = f32[256,768]{1,0:T(8,128)S(1)} fusion(bf16[256,8192]{1,0:T(8,128)(2,1)} %fusion.2, bf16[8192,768]{1,0:T(8,128)(2,1)} %bitcast.115), kind=kOutput, calls=%fused_computation.98 | convolution fusion | flops 3221225472 | bytes 17563648 | tf_op jit(solution)/shard_map/dot_general | solution.py:283
  108.6 2.4 %shard_map.73.refs_1_.a_ref = bf16[256,512]{1,0:T(8,128)(2,1)S(1)} custom-call(s32[4]{0:T(128)S(1)} %select_reduce_fusion.refs_0_, f32[256,768]{1,0:T(8,128)S(1)} %fusion.22.refs_1_, f32[256,128]{1,0:T(8,128)S(1)} %get-tuple-element.27.refs_2_, f32[256,128]{1,0:T(8,128)S(1)} %copy-done.9, bf16[4,2,256,128]{3,2,1,0:T(8,128)(2,1)S(1)} %bitcast.107), custom_call_target="tpu_custom_call" | custom-call | flops 167772160 | bytes 1310720 | tf_op jit(solution)/shard_map/pallas_call | solution.py:108
  113.2 2.8 %collective-permute-start.21 = (bf16[2,128,512]{2,1,0:T(8,128)(2,1)S(1)}, bf16[2,128,512]{2,1,0:T(8,128)(2,1)S(1)}, u32[]{:S(2)}, u32[]{:S(2)}) collective-permute-start(bf16[2,128,512]{2,1,0:T(8,128)(2,1)S(1)} %get-tuple-element.68), channel_id=1, source_target_pairs={{0,96},{1,97},{2,98},{3,99},{4,100},{5,101},{6,102},{7,103},{8,104... | collective-permute-start | bytes 786440 | tf_op jit(solution)/shard_map/ppermute | solution.py:35
  116.0 3.5 %collective-permute-start.20 = (bf16[2,128,512]{2,1,0:T(8,128)(2,1)S(1)}, bf16[2,128,512]{2,1,0:T(8,128)(2,1)S(1)}, u32[]{:S(2)}, u32[]{:S(2)}) collective-permute-start(bf16[2,128,512]{2,1,0:T(8,128)(2,1)S(1)} %slice.131), channel_id=1, source_target_pairs={{0,96},{1,97},{2,98},{3,99},{4,100},{5,101},{6,102},{7,103},{8,104... | collective-permute-start | bytes 786440 | tf_op jit(solution)/shard_map/ppermute | solution.py:35
  119.7 3.0 %collective-permute-done.21 = bf16[2,128,512]{2,1,0:T(8,128)(2,1)S(1)} collective-permute-done((bf16[2,128,512]{2,1,0:T(8,128)(2,1)S(1)}, bf16[2,128,512]{2,1,0:T(8,128)(2,1)S(1)}, u32[]{:S(2)}, u32[]{:S(2)}) %collective-permute-start.21) | collective-permute-done | bytes 262176 | tf_op jit(solution)/shard_map/ppermute | solution.py:35
  122.8 3.8 %collective-permute-start.22 = (bf16[2,128,512]{2,1,0:T(8,128)(2,1)S(1)}, bf16[2,128,512]{2,1,0:T(8,128)(2,1)S(1)}, u32[]{:S(2)}, u32[]{:S(2)}) collective-permute-start(bf16[2,128,512]{2,1,0:T(8,128)(2,1)S(1)} %add_convert_fusion.5), channel_id=1, source_target_pairs={{0,96},{1,97},{2,98},{3,99},{4,100},{5,101},{6,102},{7,103},{8,104... | collective-permute-start | bytes 786440 | tf_op jit(solution)/shard_map/ppermute | solution.py:35
  128.3 3.7 %collective-permute-done.23 = bf16[2,128,512]{2,1,0:T(8,128)(2,1)S(1)} collective-permute-done((bf16[2,128,512]{2,1,0:T(8,128)(2,1)S(1)}, bf16[2,128,512]{2,1,0:T(8,128)(2,1)S(1)}, u32[]{:S(2)}, u32[]{:S(2)}) %collective-permute-start.23) | collective-permute-done | bytes 262176 | tf_op jit(solution)/shard_map/ppermute | solution.py:35
  133.2 3.4 %collective-permute-done.19 = bf16[2,128,512]{2,1,0:T(8,128)(2,1)S(1)} collective-permute-done((bf16[2,128,512]{2,1,0:T(8,128)(2,1)S(1)}, bf16[2,128,512]{2,1,0:T(8,128)(2,1)S(1)}, u32[]{:S(2)}, u32[]{:S(2)}) %collective-permute-start.19) | collective-permute-done | bytes 262176 | tf_op jit(solution)/shard_map/ppermute | solution.py:35
  136.9 8.3 %all-gather.7.cloned.1.call-done = bf16[1,1,4096,512]{3,2,1,0:T(8,128)(2,1)} async-done(((bf16[1,1,256,512]{3,2,1,0:T(8,128)(2,1)}), bf16[1,1,4096,512]{3,2,1,0:T(8,128)(2,1)}) %all-gather.7.cloned.1.call-update) | async-done | bytes 4194320 | tf_op jit(solution)/shard_map/all_gather | solution.py:282
  147.4 2.7 %shard_map.75 = bf16[8,256,512]{2,1,0:T(8,128)(2,1)S(1)} custom-call(bf16[256,512]{1,0:T(8,128)(2,1)S(1)} %shard_map.73.refs_1_.a_ref, bf16[4096,512]{1,0:T(8,128)(2,1)S(1)} %bitcast.106), custom_call_target="tpu_custom_call" | custom-call | flops 1073741824 | bytes 6553600 | tf_op jit(solution)/shard_map/pallas_call | solution.py:186
  150.4 2.8 %collective-permute-start.29 = (bf16[2,128,512]{2,1,0:T(8,128)(2,1)S(1)}, bf16[2,128,512]{2,1,0:T(8,128)(2,1)S(1)}, u32[]{:S(2)}, u32[]{:S(2)}) collective-permute-start(bf16[2,128,512]{2,1,0:T(8,128)(2,1)S(1)} %get-tuple-element.62), channel_id=1, source_target_pairs={{0,96},{1,97},{2,98},{3,99},{4,100},{5,101},{6,102},{7,103},{8,104... | collective-permute-start | bytes 786440 | tf_op jit(solution)/shard_map/ppermute | solution.py:35
  153.2 3.3 %collective-permute-start.28 = (bf16[2,128,512]{2,1,0:T(8,128)(2,1)S(1)}, bf16[2,128,512]{2,1,0:T(8,128)(2,1)S(1)}, u32[]{:S(2)}, u32[]{:S(2)}) collective-permute-start(bf16[2,128,512]{2,1,0:T(8,128)(2,1)S(1)} %slice.140), channel_id=1, source_target_pairs={{0,96},{1,97},{2,98},{3,99},{4,100},{5,101},{6,102},{7,103},{8,104... | collective-permute-start | bytes 786440 | tf_op jit(solution)/shard_map/ppermute | solution.py:35
  156.6 3.2 %collective-permute-done.29 = bf16[2,128,512]{2,1,0:T(8,128)(2,1)S(1)} collective-permute-done((bf16[2,128,512]{2,1,0:T(8,128)(2,1)S(1)}, bf16[2,128,512]{2,1,0:T(8,128)(2,1)S(1)}, u32[]{:S(2)}, u32[]{:S(2)}) %collective-permute-start.29) | collective-permute-done | bytes 262176 | tf_op jit(solution)/shard_map/ppermute | solution.py:35
  159.9 3.8 %collective-permute-start.30 = (bf16[2,128,512]{2,1,0:T(8,128)(2,1)S(1)}, bf16[2,128,512]{2,1,0:T(8,128)(2,1)S(1)}, u32[]{:S(2)}, u32[]{:S(2)}) collective-permute-start(bf16[2,128,512]{2,1,0:T(8,128)(2,1)S(1)} %add_convert_fusion.1), channel_id=1, source_target_pairs={{0,96},{1,97},{2,98},{3,99},{4,100},{5,101},{6,102},{7,103},{8,104... | collective-permute-start | bytes 786440 | tf_op jit(solution)/shard_map/ppermute | solution.py:35
  165.5 2.7 %collective-permute-start.25 = (bf16[256,512]{1,0:T(8,128)(2,1)S(1)}, bf16[256,512]{1,0:T(8,128)(2,1)S(1)}, u32[]{:S(2)}, u32[]{:S(2)}) collective-permute-start(bf16[256,512]{1,0:T(8,128)(2,1)S(1)} %get-tuple-element.56), channel_id=1, source_target_pairs={{0,144},{1,145},{2,146},{3,147},{4,148},{5,149},{6,150},{7,151},{8... | collective-permute-start | bytes 786440 | tf_op jit(solution)/shard_map/ppermute | solution.py:35
  170.4 3.4 %collective-permute-done.27 = bf16[2,128,512]{2,1,0:T(8,128)(2,1)S(1)} collective-permute-done((bf16[2,128,512]{2,1,0:T(8,128)(2,1)S(1)}, bf16[2,128,512]{2,1,0:T(8,128)(2,1)S(1)}, u32[]{:S(2)}, u32[]{:S(2)}) %collective-permute-start.27) | collective-permute-done | bytes 262176 | tf_op jit(solution)/shard_map/ppermute | solution.py:35
  177.9 3.6 %collective-permute-done.32 = bf16[256,512]{1,0:T(8,128)(2,1)S(1)} collective-permute-done((bf16[256,512]{1,0:T(8,128)(2,1)S(1)}, bf16[256,512]{1,0:T(8,128)(2,1)S(1)}, u32[]{:S(2)}, u32[]{:S(2)}) %collective-permute-start.32) | collective-permute-done | bytes 262176 | tf_op jit(solution)/shard_map/ppermute | solution.py:35
  181.5 2.4 %collective-permute-done.33 = bf16[256,512]{1,0:T(8,128)(2,1)S(1)} collective-permute-done((bf16[256,512]{1,0:T(8,128)(2,1)S(1)}, bf16[256,512]{1,0:T(8,128)(2,1)S(1)}, u32[]{:S(2)}, u32[]{:S(2)}) %collective-permute-start.33) | collective-permute-done | bytes 262176 | tf_op jit(solution)/shard_map/ppermute | solution.py:35
  (143 shorter events, 51.8 us)
Async XLA Ops:
  6.5 93.1 %all-gather.5.cloned.1.call-start = ((), (), s32[]{:S(2)}) async-start(), calls=%async_computation | async-start | bytes 13369344 | tf_op jit(solution)/shard_map/all_gather | solution.py:248
  7.3 138.0 %all-gather.7.cloned.1.call-start = ((), (), s32[]{:S(2)}) async-start(), calls=%async_computation.1 | async-start | bytes 4456448 | tf_op jit(solution)/shard_map/all_gather | solution.py:282
  9.1 16.0 %collective-permute-start.9 = (bf16[256,512]{1,0:T(8,128)(2,1)S(1)}, bf16[256,512]{1,0:T(8,128)(2,1)S(1)}, u32[]{:S(2)}, u32[]{:S(2)}) collective-permute-start(bf16[256,512]{1,0:T(8,128)(2,1)S(1)} %get-tuple-element.30.refs_2_), channel_id=1, source_target_pairs={{0,2},{1,3},{2,4},{3,5},{4,6},{5,7},{6,8},{7,9},{8,10},{9,11},{10,... | collective-permute-start | bytes 786440 | tf_op jit(solution)/shard_map/ppermute | solution.py:35
  11.0 14.6 %collective-permute-start.8 = (bf16[256,512]{1,0:T(8,128)(2,1)S(1)}, bf16[256,512]{1,0:T(8,128)(2,1)S(1)}, u32[]{:S(2)}, u32[]{:S(2)}) collective-permute-start(bf16[256,512]{1,0:T(8,128)(2,1)S(1)} %get-tuple-element.30.refs_2_), channel_id=1, source_target_pairs={{0,14},{1,15},{2,0},{3,1},{4,2},{5,3},{6,4},{7,5},{8,6},{9,7},{10,... | collective-permute-start | bytes 786440 | tf_op jit(solution)/shard_map/ppermute | solution.py:35
  11.1 24.4 %collective-permute-start.5 = (bf16[1,4,2,1,256,128]{5,4,2,1,3,0:T(8,128)(2,1)}, bf16[1,4,2,1,256,128]{5,4,2,1,3,0:T(8,128)(2,1)S(1)}, u32[]{:S(2)}, u32[]{:S(2)}) collective-permute-start(bf16[1,4,2,1,256,128]{5,4,2,1,3,0:T(8,128)(2,1)} %bitcast.112), channel_id=1, source_target_pairs={{0,1},{1,2},{2,3},{3,4},{4,5},{5,6},{6,7},{7,8},{8,9},{9,10},{10,1... | collective-permute-start | bytes 1572872 | tf_op jit(solution)/shard_map/ppermute | solution.py:152
  11.1 28.3 %collective-permute-start.6 = (bf16[1,4,2,1,256,128]{5,4,2,1,3,0:T(8,128)(2,1)}, bf16[1,4,2,1,256,128]{5,4,2,1,3,0:T(8,128)(2,1)S(1)}, u32[]{:S(2)}, u32[]{:S(2)}) collective-permute-start(bf16[1,4,2,1,256,128]{5,4,2,1,3,0:T(8,128)(2,1)} %bitcast.113), channel_id=1, source_target_pairs={{1,0},{2,1},{3,2},{4,3},{5,4},{6,5},{7,6},{8,7},{9,8},{10,9},{11,1... | collective-permute-start | bytes 1572872 | tf_op jit(solution)/shard_map/ppermute | solution.py:153
  14.2 16.0 %collective-permute-start = (bf16[256,1024]{1,0:T(8,128)(2,1)}, bf16[256,1024]{1,0:T(8,128)(2,1)S(1)}, u32[]{:S(2)}, u32[]{:S(2)}) collective-permute-start(bf16[256,1024]{1,0:T(8,128)(2,1)} %bitcast.1), channel_id=1, source_target_pairs={{0,16},{1,17},{2,18},{3,19},{4,20},{5,21},{6,22},{7,23},{8,24},{9,... | collective-permute-start | bytes 1572872 | tf_op jit(solution)/shard_map/ppermute | solution.py:35
  25.1 61.8 %collective-permute-start.7 = (bf16[256,1024]{1,0:T(8,128)(2,1)}, bf16[256,1024]{1,0:T(8,128)(2,1)}, u32[]{:S(2)}, u32[]{:S(2)}) collective-permute-start(bf16[256,1024]{1,0:T(8,128)(2,1)} %bitcast.1), channel_id=1, source_target_pairs={{0,128},{1,129},{2,130},{3,131},{4,132},{5,133},{6,134},{7,135},{8... | collective-permute-start | bytes 1572872 | tf_op jit(solution)/shard_map/ppermute | solution.py:35
  25.7 16.3 %collective-permute-start.11 = (bf16[256,512]{1,0:T(8,128)(2,1)S(1)}, bf16[256,512]{1,0:T(8,128)(2,1)S(1)}, u32[]{:S(2)}, u32[]{:S(2)}) collective-permute-start(bf16[256,512]{1,0:T(8,128)(2,1)S(1)} %collective-permute-done.9.refs_4_), channel_id=1, source_target_pairs={{0,2},{1,3},{2,4},{3,5},{4,6},{5,7},{6,8},{7,9},{8,10},{9,11},{10,... | collective-permute-start | bytes 786440 | tf_op jit(solution)/shard_map/ppermute | solution.py:35
  30.2 14.3 %collective-permute-start.10 = (bf16[256,512]{1,0:T(8,128)(2,1)S(1)}, bf16[256,512]{1,0:T(8,128)(2,1)S(1)}, u32[]{:S(2)}, u32[]{:S(2)}) collective-permute-start(bf16[256,512]{1,0:T(8,128)(2,1)S(1)} %collective-permute-done.8.refs_3_), channel_id=1, source_target_pairs={{0,14},{1,15},{2,0},{3,1},{4,2},{5,3},{6,4},{7,5},{8,6},{9,7},{10,... | collective-permute-start | bytes 786440 | tf_op jit(solution)/shard_map/ppermute | solution.py:35
  35.5 35.0 %collective-permute-start.1 = (bf16[2,256,1024]{2,1,0:T(8,128)(2,1)}, bf16[2,256,1024]{2,1,0:T(8,128)(2,1)}, u32[]{:S(2)}, u32[]{:S(2)}) collective-permute-start(bf16[2,256,1024]{2,1,0:T(8,128)(2,1)} %pad_maximum_fusion), channel_id=1, source_target_pairs={{0,96},{1,97},{2,98},{3,99},{4,100},{5,101},{6,102},{7,103},{8,104... | collective-permute-start | bytes 3145736 | tf_op jit(solution)/shard_map/ppermute | solution.py:35
  39.5 28.4 %collective-permute-start.2 = (bf16[2,256,1024]{2,1,0:T(8,128)(2,1)}, bf16[2,256,1024]{2,1,0:T(8,128)(2,1)}, u32[]{:S(2)}, u32[]{:S(2)}) collective-permute-start(bf16[2,256,1024]{2,1,0:T(8,128)(2,1)} %pad_maximum_fusion), channel_id=1, source_target_pairs={{0,32},{1,33},{2,34},{3,35},{4,36},{5,37},{6,38},{7,39},{8,40},{9,... | collective-permute-start | bytes 3145736 | tf_op jit(solution)/shard_map/ppermute | solution.py:35
  42.0 13.6 %collective-permute-start.13 = (bf16[256,512]{1,0:T(8,128)(2,1)S(1)}, bf16[256,512]{1,0:T(8,128)(2,1)S(1)}, u32[]{:S(2)}, u32[]{:S(2)}) collective-permute-start(bf16[256,512]{1,0:T(8,128)(2,1)S(1)} %collective-permute-done.11.refs_6_), channel_id=1, source_target_pairs={{0,2},{1,3},{2,4},{3,5},{4,6},{5,7},{6,8},{7,9},{8,10},{9,11},{10,... | collective-permute-start | bytes 786440 | tf_op jit(solution)/shard_map/ppermute | solution.py:35
  44.5 15.2 %collective-permute-start.12 = (bf16[256,512]{1,0:T(8,128)(2,1)S(1)}, bf16[256,512]{1,0:T(8,128)(2,1)S(1)}, u32[]{:S(2)}, u32[]{:S(2)}) collective-permute-start(bf16[256,512]{1,0:T(8,128)(2,1)S(1)} %collective-permute-done.10.refs_5_), channel_id=1, source_target_pairs={{0,14},{1,15},{2,0},{3,1},{4,2},{5,3},{6,4},{7,5},{8,6},{9,7},{10,... | collective-permute-start | bytes 786440 | tf_op jit(solution)/shard_map/ppermute | solution.py:35
  59.8 28.0 %collective-permute-start.16 = (bf16[5,256,512]{2,1,0:T(8,128)(2,1)S(1)}, bf16[5,256,512]{2,1,0:T(8,128)(2,1)S(1)}, u32[]{:S(2)}, u32[]{:S(2)}) collective-permute-start(bf16[5,256,512]{2,1,0:T(8,128)(2,1)S(1)} %bitcast_dynamic-update-slice_fusion.10), channel_id=1, source_target_pairs={{0,1},{1,0},{2,3},{3,2},{4,5},{5,4},{6,7},{7,6},{8,9},{9,8},{10,11... | collective-permute-start | bytes 3932168 | tf_op jit(solution)/shard_map/ppermute | solution.py:35
  68.9 10.5 %collective-permute-start.3 = (bf16[256,1024]{1,0:T(8,128)(2,1)S(1)}, bf16[256,1024]{1,0:T(8,128)(2,1)S(1)}, u32[]{:S(2)}, u32[]{:S(2)}) collective-permute-start(bf16[256,1024]{1,0:T(8,128)(2,1)S(1)} %slice_bitcast_fusion.1), channel_id=1, source_target_pairs={{0,32},{1,33},{2,34},{3,35},{4,36},{5,37},{6,38},{7,39},{8,40},{9,... | collective-permute-start | bytes 1572872 | tf_op jit(solution)/shard_map/ppermute | solution.py:35
  71.7 9.3 %collective-permute-start.4 = (bf16[256,1024]{1,0:T(8,128)(2,1)S(1)}, bf16[256,1024]{1,0:T(8,128)(2,1)S(1)}, u32[]{:S(2)}, u32[]{:S(2)}) collective-permute-start(bf16[256,1024]{1,0:T(8,128)(2,1)S(1)} %slice_bitcast_fusion), channel_id=1, source_target_pairs={{0,96},{1,97},{2,98},{3,99},{4,100},{5,101},{6,102},{7,103},{8,104... | collective-permute-start | bytes 1572872 | tf_op jit(solution)/shard_map/ppermute | solution.py:35
  73.5 13.3 %collective-permute-start.17 = (bf16[3,256,512]{2,1,0:T(8,128)(2,1)S(1)}, bf16[3,256,512]{2,1,0:T(8,128)(2,1)S(1)}, u32[]{:S(2)}, u32[]{:S(2)}) collective-permute-start(bf16[3,256,512]{2,1,0:T(8,128)(2,1)S(1)} %pad_maximum_fusion.1), channel_id=1, source_target_pairs={{0,1},{1,0},{2,3},{3,2},{4,5},{5,4},{6,7},{7,6},{8,9},{9,8},{10,11... | collective-permute-start | bytes 2359304 | tf_op jit(solution)/shard_map/ppermute | solution.py:35
  113.2 9.5 %collective-permute-start.21 = (bf16[2,128,512]{2,1,0:T(8,128)(2,1)S(1)}, bf16[2,128,512]{2,1,0:T(8,128)(2,1)S(1)}, u32[]{:S(2)}, u32[]{:S(2)}) collective-permute-start(bf16[2,128,512]{2,1,0:T(8,128)(2,1)S(1)} %get-tuple-element.68), channel_id=1, source_target_pairs={{0,96},{1,97},{2,98},{3,99},{4,100},{5,101},{6,102},{7,103},{8,104... | collective-permute-start | bytes 786440 | tf_op jit(solution)/shard_map/ppermute | solution.py:35
  116.0 10.5 %collective-permute-start.18 = (bf16[2,128,512]{2,1,0:T(8,128)(2,1)S(1)}, bf16[2,128,512]{2,1,0:T(8,128)(2,1)S(1)}, u32[]{:S(2)}, u32[]{:S(2)}) collective-permute-start(bf16[2,128,512]{2,1,0:T(8,128)(2,1)S(1)} %get-tuple-element.67), channel_id=1, source_target_pairs={{0,32},{1,33},{2,34},{3,35},{4,36},{5,37},{6,38},{7,39},{8,40},{9,... | collective-permute-start | bytes 786440 | tf_op jit(solution)/shard_map/ppermute | solution.py:35
  116.0 12.3 %collective-permute-start.20 = (bf16[2,128,512]{2,1,0:T(8,128)(2,1)S(1)}, bf16[2,128,512]{2,1,0:T(8,128)(2,1)S(1)}, u32[]{:S(2)}, u32[]{:S(2)}) collective-permute-start(bf16[2,128,512]{2,1,0:T(8,128)(2,1)S(1)} %slice.131), channel_id=1, source_target_pairs={{0,96},{1,97},{2,98},{3,99},{4,100},{5,101},{6,102},{7,103},{8,104... | collective-permute-start | bytes 786440 | tf_op jit(solution)/shard_map/ppermute | solution.py:35
  119.6 12.4 %collective-permute-start.23 = (bf16[2,128,512]{2,1,0:T(8,128)(2,1)S(1)}, bf16[2,128,512]{2,1,0:T(8,128)(2,1)S(1)}, u32[]{:S(2)}, u32[]{:S(2)}) collective-permute-start(bf16[2,128,512]{2,1,0:T(8,128)(2,1)S(1)} %slice.135), channel_id=1, source_target_pairs={{0,32},{1,33},{2,34},{3,35},{4,36},{5,37},{6,38},{7,39},{8,40},{9,... | collective-permute-start | bytes 786440 | tf_op jit(solution)/shard_map/ppermute | solution.py:35
  122.8 10.5 %collective-permute-start.22 = (bf16[2,128,512]{2,1,0:T(8,128)(2,1)S(1)}, bf16[2,128,512]{2,1,0:T(8,128)(2,1)S(1)}, u32[]{:S(2)}, u32[]{:S(2)}) collective-permute-start(bf16[2,128,512]{2,1,0:T(8,128)(2,1)S(1)} %add_convert_fusion.5), channel_id=1, source_target_pairs={{0,96},{1,97},{2,98},{3,99},{4,100},{5,101},{6,102},{7,103},{8,104... | collective-permute-start | bytes 786440 | tf_op jit(solution)/shard_map/ppermute | solution.py:35
  126.6 10.0 %collective-permute-start.19 = (bf16[2,128,512]{2,1,0:T(8,128)(2,1)S(1)}, bf16[2,128,512]{2,1,0:T(8,128)(2,1)S(1)}, u32[]{:S(2)}, u32[]{:S(2)}) collective-permute-start(bf16[2,128,512]{2,1,0:T(8,128)(2,1)S(1)} %add_convert_fusion.7), channel_id=1, source_target_pairs={{0,32},{1,33},{2,34},{3,35},{4,36},{5,37},{6,38},{7,39},{8,40},{9,... | collective-permute-start | bytes 786440 | tf_op jit(solution)/shard_map/ppermute | solution.py:35
  150.4 9.5 %collective-permute-start.29 = (bf16[2,128,512]{2,1,0:T(8,128)(2,1)S(1)}, bf16[2,128,512]{2,1,0:T(8,128)(2,1)S(1)}, u32[]{:S(2)}, u32[]{:S(2)}) collective-permute-start(bf16[2,128,512]{2,1,0:T(8,128)(2,1)S(1)} %get-tuple-element.62), channel_id=1, source_target_pairs={{0,96},{1,97},{2,98},{3,99},{4,100},{5,101},{6,102},{7,103},{8,104... | collective-permute-start | bytes 786440 | tf_op jit(solution)/shard_map/ppermute | solution.py:35
  153.2 10.5 %collective-permute-start.26 = (bf16[2,128,512]{2,1,0:T(8,128)(2,1)S(1)}, bf16[2,128,512]{2,1,0:T(8,128)(2,1)S(1)}, u32[]{:S(2)}, u32[]{:S(2)}) collective-permute-start(bf16[2,128,512]{2,1,0:T(8,128)(2,1)S(1)} %get-tuple-element.61), channel_id=1, source_target_pairs={{0,32},{1,33},{2,34},{3,35},{4,36},{5,37},{6,38},{7,39},{8,40},{9,... | collective-permute-start | bytes 786440 | tf_op jit(solution)/shard_map/ppermute | solution.py:35
  153.2 12.3 %collective-permute-start.28 = (bf16[2,128,512]{2,1,0:T(8,128)(2,1)S(1)}, bf16[2,128,512]{2,1,0:T(8,128)(2,1)S(1)}, u32[]{:S(2)}, u32[]{:S(2)}) collective-permute-start(bf16[2,128,512]{2,1,0:T(8,128)(2,1)S(1)} %slice.140), channel_id=1, source_target_pairs={{0,96},{1,97},{2,98},{3,99},{4,100},{5,101},{6,102},{7,103},{8,104... | collective-permute-start | bytes 786440 | tf_op jit(solution)/shard_map/ppermute | solution.py:35
  156.5 12.7 %collective-permute-start.31 = (bf16[2,128,512]{2,1,0:T(8,128)(2,1)S(1)}, bf16[2,128,512]{2,1,0:T(8,128)(2,1)S(1)}, u32[]{:S(2)}, u32[]{:S(2)}) collective-permute-start(bf16[2,128,512]{2,1,0:T(8,128)(2,1)S(1)} %slice.144), channel_id=1, source_target_pairs={{0,32},{1,33},{2,34},{3,35},{4,36},{5,37},{6,38},{7,39},{8,40},{9,... | collective-permute-start | bytes 786440 | tf_op jit(solution)/shard_map/ppermute | solution.py:35
  159.9 10.5 %collective-permute-start.30 = (bf16[2,128,512]{2,1,0:T(8,128)(2,1)S(1)}, bf16[2,128,512]{2,1,0:T(8,128)(2,1)S(1)}, u32[]{:S(2)}, u32[]{:S(2)}) collective-permute-start(bf16[2,128,512]{2,1,0:T(8,128)(2,1)S(1)} %add_convert_fusion.1), channel_id=1, source_target_pairs={{0,96},{1,97},{2,98},{3,99},{4,100},{5,101},{6,102},{7,103},{8,104... | collective-permute-start | bytes 786440 | tf_op jit(solution)/shard_map/ppermute | solution.py:35
  163.8 10.0 %collective-permute-start.27 = (bf16[2,128,512]{2,1,0:T(8,128)(2,1)S(1)}, bf16[2,128,512]{2,1,0:T(8,128)(2,1)S(1)}, u32[]{:S(2)}, u32[]{:S(2)}) collective-permute-start(bf16[2,128,512]{2,1,0:T(8,128)(2,1)S(1)} %add_convert_fusion.3), channel_id=1, source_target_pairs={{0,32},{1,33},{2,34},{3,35},{4,36},{5,37},{6,38},{7,39},{8,40},{9,... | collective-permute-start | bytes 786440 | tf_op jit(solution)/shard_map/ppermute | solution.py:35
  163.9 13.8 %collective-permute-start.24 = (bf16[256,512]{1,0:T(8,128)(2,1)S(1)}, bf16[256,512]{1,0:T(8,128)(2,1)S(1)}, u32[]{:S(2)}, u32[]{:S(2)}) collective-permute-start(bf16[256,512]{1,0:T(8,128)(2,1)S(1)} %get-tuple-element.55), channel_id=1, source_target_pairs={{0,128},{1,129},{2,130},{3,131},{4,132},{5,133},{6,134},{7,135},{8... | collective-permute-start | bytes 786440 | tf_op jit(solution)/shard_map/ppermute | solution.py:35
  165.5 12.3 %collective-permute-start.25 = (bf16[256,512]{1,0:T(8,128)(2,1)S(1)}, bf16[256,512]{1,0:T(8,128)(2,1)S(1)}, u32[]{:S(2)}, u32[]{:S(2)}) collective-permute-start(bf16[256,512]{1,0:T(8,128)(2,1)S(1)} %get-tuple-element.56), channel_id=1, source_target_pairs={{0,144},{1,145},{2,146},{3,147},{4,148},{5,149},{6,150},{7,151},{8... | collective-permute-start | bytes 786440 | tf_op jit(solution)/shard_map/ppermute | solution.py:35
  (19 other events, 203.3 us)
Sparse Core Ops, SparseCore 0:
  9.2 90.4 all-gather.4
  101.5 43.7 all-gather.6

commit v2 on v1

--- a/solution.py
+++ b/solution.py
@@ -300,29 +300,26 @@
         far_up, far_down = send(far_up, dy=1), send(far_down, dy=-1)
         up_low, up_high = low_high(1)
         down_low, down_high = low_high(-1)
-        direct_up, direct_down = send(up_high, dy=1), send(down_low, dy=-1)
-        relayed_up = send(
-            (up_low.astype(jnp.float32) + far_up.astype(jnp.float32)).astype(jnp.bfloat16), dy=1
-        )
-        relayed_down = send(
-            (down_high.astype(jnp.float32) + far_down.astype(jnp.float32)).astype(jnp.bfloat16),
-            dy=-1,
-        )
+        relay_up = (up_low.astype(jnp.float32) + far_up.astype(jnp.float32)).astype(jnp.bfloat16)
+        relay_down = (down_high.astype(jnp.float32) + far_down.astype(jnp.float32)).astype(
+            jnp.bfloat16
+        )
+        if half == 0:
+            direct_up, direct_down = send(up_high, dy=1), send(down_low, dy=-1)
+            from_below = jnp.concatenate([send(relay_up, dy=1), direct_up], axis=1)
+            from_above = jnp.concatenate([direct_down, send(relay_down, dy=-1)], axis=1)
+        else:
+            from_below = send(jnp.concatenate([relay_up, up_high], axis=1), dy=1)
+            from_above = send(jnp.concatenate([down_low, relay_down], axis=1), dy=-1)
         here_low, here_high = low_high(0)
-        low = (
-            here_low.astype(jnp.float32)
-            + relayed_up.astype(jnp.float32)
-            + direct_down.astype(jnp.float32)
-        )
-        high = (
-            here_high.astype(jnp.float32)
-            + relayed_down.astype(jnp.float32)
-            + direct_up.astype(jnp.float32)
-        )
-        summed = jnp.concatenate([low, high], axis=1).astype(jnp.bfloat16)
-        attended, summed = lax.optimization_barrier((attended, summed))
+        summed = (
+            jnp.concatenate([here_low, here_high], axis=1).astype(jnp.float32)
+            + from_below.astype(jnp.float32)
+            + from_above.astype(jnp.float32)
+        ).astype(jnp.bfloat16)
         same = send(jnp.where(xh == 0, summed[0], summed[1]), ds=1)
         cross = send(jnp.where(xh == 0, summed[1], summed[0]), ds=1, dxh=1)
+        attended, same, cross = lax.optimization_barrier((attended, same, cross))
         results.append(same.astype(jnp.float32) + cross.astype(jnp.float32))
     summed = jnp.concatenate(
         [r[:, k * rows : (k + 1) * rows] for k in range(NC) for r in results], axis=1

time: 194 us -> 194 us (level)
  starting transfers between devices: 53.3 us -> 48.6 us
  local copies, waits for them, and re-layouts: 18.3 us -> 21.9 us
    all_gather x1, waiting for transfers between devices: 8.33 us -> 0.01 us  [body(): second = lax.all_gather(w_out[0, 0, rows:], 'particle', axis=0, tiled=True)]
    ppermute x32 -> x30, waiting for transfers between devices: 55.7 us -> 63.9 us  [send(): return lax.ppermute(value, AXES, moves(**shift))]
    ppermute x32 -> x30, starting transfers between devices: 50.1 us -> 45.5 us  [send(): return lax.ppermute(value, AXES, moves(**shift))]
    unnamed x48 -> x52, local copies, waits for them, and re-layouts: 10 us -> 11.4 us
  transfers between devices with their start and end apart: 36 -> 34, of which waited for: 20 -> 18; matrix products, arithmetic and copies ran while one was open for 19% -> 21% of each run, Pallas kernels for 2% -> 2%
where the time goes in v2:
time: 194 us; the launch traced here: 192 us
  waiting for transfers between devices  75.4 us (39%)
  starting transfers between devices  48.6 us (25%)
  local copies, waits for them, and re-layouts  21.9 us (11%)
  between operations  14.2 us (7%)
  other arithmetic  13.3 us (7%)
  matrix products  11.4 us (6%)
  Pallas kernels  7.08 us (4%)
    ppermute x30, waiting for transfers between devices, send(): return lax.ppermute(value, AXES, moves(**shift))  63.9 us
    ppermute x30, starting transfers between devices, send(): return lax.ppermute(value, AXES, moves(**shift))  45.5 us
    unnamed x52, local copies, waits for them, and re-layouts  11.4 us
    all_gather x1, waiting for transfers between devices, body(): w_full = lax.all_gather(w_qkv[0, 0], 'particle', axis=0, tiled=True)  10.7 us
    dot_general x1, matrix products, body(): projected = jnp.dot(normed, w_full, preferred_element_type=jnp.float32)  8.96 us
  transfers between devices with their start and end apart: 34, of which 18 were waited for; matrix products, arithmetic and copies ran while one was open for 21% of the time, Pallas kernels for 2%

profile of v2, /device:TPU:32, one launch (start us, length us, event | category | flops | bytes accessed | tf_op | source)
XLA Modules:
  0.0 191.8 jit_solution(7107182587484866544)
XLA Ops:
  11.1 3.1 %collective-permute-start.6 = (bf16[1,4,2,1,256,128]{5,4,2,1,3,0:T(8,128)(2,1)}, bf16[1,4,2,1,256,128]{5,4,2,1,3,0:T(8,128)(2,1)S(1)}, u32[]{:S(2)}, u32[]{:S(2)}) collective-permute-start(bf16[1,4,2,1,256,128]{5,4,2,1,3,0:T(8,128)(2,1)} %bitcast.117), channel_id=1, source_target_pairs={{1,0},{2,1},{3,2},{4,3},{5,4},{6,5},{7,6},{8,7},{9,8},{10,9},{11,1... | collective-permute-start | bytes 1572872 | tf_op jit(solution)/shard_map/ppermute | solution.py:153
  14.2 3.0 %collective-permute-start = (bf16[256,1024]{1,0:T(8,128)(2,1)}, bf16[256,1024]{1,0:T(8,128)(2,1)S(1)}, u32[]{:S(2)}, u32[]{:S(2)}) collective-permute-start(bf16[256,1024]{1,0:T(8,128)(2,1)} %bitcast.1), channel_id=1, source_target_pairs={{0,16},{1,17},{2,18},{3,19},{4,20},{5,21},{6,22},{7,23},{8,24},{9,... | collective-permute-start | bytes 1572872 | tf_op jit(solution)/shard_map/ppermute | solution.py:35
  26.6 4.2 %collective-permute-done = bf16[256,1024]{1,0:T(8,128)(2,1)S(1)} collective-permute-done((bf16[256,1024]{1,0:T(8,128)(2,1)}, bf16[256,1024]{1,0:T(8,128)(2,1)S(1)}, u32[]{:S(2)}, u32[]{:S(2)}) %collective-permute-start) | collective-permute-done | bytes 524320 | tf_op jit(solution)/shard_map/ppermute | solution.py:35
  30.8 3.1 %collective-permute-start.10 = (bf16[256,512]{1,0:T(8,128)(2,1)S(1)}, bf16[256,512]{1,0:T(8,128)(2,1)S(1)}, u32[]{:S(2)}, u32[]{:S(2)}) collective-permute-start(bf16[256,512]{1,0:T(8,128)(2,1)S(1)} %collective-permute-done.8.refs_3_), channel_id=1, source_target_pairs={{0,14},{1,15},{2,0},{3,1},{4,2},{5,3},{6,4},{7,5},{8,6},{9,7},{10,... | collective-permute-start | bytes 786440 | tf_op jit(solution)/shard_map/ppermute | solution.py:35
  33.9 2.1 %pad_maximum_fusion = bf16[2,256,1024]{2,1,0:T(8,128)(2,1)} fusion(bf16[1,256,1024]{2,1,0:T(8,128)(2,1)S(1)} %bitcast.115, bf16[1,256,1024]{2,1,0:T(8,128)(2,1)} %param.7), kind=kLoop, calls=%fused_computation.12 | loop fusion | flops 524288 | bytes 2097152 | tf_op jit(solution)/shard_map/stack | solution.py:250
  36.0 3.0 %collective-permute-start.1 = (bf16[2,256,1024]{2,1,0:T(8,128)(2,1)}, bf16[2,256,1024]{2,1,0:T(8,128)(2,1)}, u32[]{:S(2)}, u32[]{:S(2)}) collective-permute-start(bf16[2,256,1024]{2,1,0:T(8,128)(2,1)} %pad_maximum_fusion), channel_id=1, source_target_pairs={{0,96},{1,97},{2,98},{3,99},{4,100},{5,101},{6,102},{7,103},{8,104... | collective-permute-start | bytes 3145736 | tf_op jit(solution)/shard_map/ppermute | solution.py:35
  42.1 2.4 %fusion.7 = bf16[1,4,512,128]{3,1,2,0:T(4,128)(2,1)S(1)} fusion(bf16[1,4,65536]{2,1,0:T(4,128)(2,1)} %concatenate.47, bf16[1,4,65536]{2,1,0:T(4,128)(2,1)S(1)} %concatenate.46, bf16[1,4,65536]{2,1,0:T(4,128)(2,1)} %concatenate.45, s32[4]{0:T(128)S(1)} %fusion.16), kind=kOutput, calls=%fused_computation.11 | convolution fusion | flops 11272240 | bytes 2097168 | tf_op jit(solution)/shard_map/jk,lkr->ljr/dot_general | solution.py:128
  46.9 11.1 %collective-permute-done.13.refs_8_ = bf16[256,512]{1,0:T(8,128)(2,1)S(1)} collective-permute-done((bf16[256,512]{1,0:T(8,128)(2,1)S(1)}, bf16[256,512]{1,0:T(8,128)(2,1)S(1)}, u32[]{:S(2)}, u32[]{:S(2)}) %collective-permute-start.13) | collective-permute-done | bytes 262176 | tf_op jit(solution)/shard_map/ppermute | solution.py:35
  59.5 7.1 %collective-permute-done.14 = bf16[128,512]{1,0:T(8,128)(2,1)S(1)} collective-permute-done((bf16[128,512]{1,0:T(8,128)(2,1)S(1)}, bf16[128,512]{1,0:T(8,128)(2,1)S(1)}, u32[]{:S(2)}, u32[]{:S(2)}) %collective-permute-start.14) | collective-permute-done | bytes 131104 | tf_op jit(solution)/shard_map/ppermute | solution.py:35
  66.6 3.2 %collective-permute-start.15 = (bf16[128,512]{1,0:T(8,128)(2,1)S(1)}, bf16[128,512]{1,0:T(8,128)(2,1)S(1)}, u32[]{:S(2)}, u32[]{:S(2)}) collective-permute-start(bf16[128,512]{1,0:T(8,128)(2,1)S(1)} %slice.117), channel_id=1, source_target_pairs={{0,14},{1,15},{2,0},{3,1},{4,2},{5,3},{6,4},{7,5},{8,6},{9,7},{10,... | collective-permute-start | bytes 393224 | tf_op jit(solution)/shard_map/ppermute | solution.py:35
  72.6 2.8 %collective-permute-start.4 = (bf16[256,1024]{1,0:T(8,128)(2,1)S(1)}, bf16[256,1024]{1,0:T(8,128)(2,1)S(1)}, u32[]{:S(2)}, u32[]{:S(2)}) collective-permute-start(bf16[256,1024]{1,0:T(8,128)(2,1)S(1)} %slice_bitcast_fusion), channel_id=1, source_target_pairs={{0,96},{1,97},{2,98},{3,99},{4,100},{5,101},{6,102},{7,103},{8,104... | collective-permute-start | bytes 1572872 | tf_op jit(solution)/shard_map/ppermute | solution.py:35
  76.9 4.5 %collective-permute-done.3 = bf16[256,1024]{1,0:T(8,128)(2,1)S(1)} collective-permute-done((bf16[256,1024]{1,0:T(8,128)(2,1)S(1)}, bf16[256,1024]{1,0:T(8,128)(2,1)S(1)}, u32[]{:S(2)}, u32[]{:S(2)}) %collective-permute-start.3) | collective-permute-done | bytes 524320 | tf_op jit(solution)/shard_map/ppermute | solution.py:35
  84.8 3.2 %fusion.2 = bf16[256,8192]{1,0:T(8,128)(2,1)} fusion(bf16[256,8192]{1,0:T(8,128)(2,1)S(1)} %bitcast_dynamic-update-slice_fusion, f32[8192]{0:T(1024)S(1)} %bitcast.118, f32[256]{0:T(256)S(1)} %add_rsqrt_fusion), kind=kLoop, calls=%fused_computation.5 | loop fusion | flops 8388608 | bytes 8422400 | tf_op jit(solution)/shard_map/convert_element_type | solution.py:267
  88.9 10.7 %all-gather.5.cloned.1.call-done = bf16[1,1,8192,768]{3,2,1,0:T(8,128)(2,1)} async-done(((bf16[1,1,512,768]{3,2,1,0:T(8,128)(2,1)}), bf16[1,1,8192,768]{3,2,1,0:T(8,128)(2,1)}) %all-gather.5.cloned.1.call-update) | async-done | bytes 12582928 | tf_op jit(solution)/shard_map/all_gather | solution.py:248
  99.7 9.0 %fusion.26.refs_1_ = f32[256,768]{1,0:T(8,128)S(1)} fusion(bf16[256,8192]{1,0:T(8,128)(2,1)} %fusion.2, bf16[8192,768]{1,0:T(8,128)(2,1)} %bitcast.119), kind=kOutput, calls=%fused_computation.98 | convolution fusion | flops 3221225472 | bytes 17563648 | tf_op jit(solution)/shard_map/dot_general | solution.py:283
  108.6 2.4 %shard_map.73.refs_1_.a_ref = bf16[256,512]{1,0:T(8,128)(2,1)S(1)} custom-call(s32[4]{0:T(128)S(1)} %select_reduce_fusion.refs_0_, f32[256,768]{1,0:T(8,128)S(1)} %fusion.26.refs_1_, f32[256,128]{1,0:T(8,128)S(1)} %get-tuple-element.29.refs_2_, f32[256,128]{1,0:T(8,128)S(1)} %get-tuple-element.30.refs_3_, bf16[4,2,256,128]{3,2,1,0:T(8,128)(2,1)S(1)} %bitcast.111), custom_call_target="tpu_custom_call" | custom-call | flops 167772160 | bytes 1310720 | tf_op jit(solution)/shard_map/pallas_call | solution.py:108
  114.5 2.8 %collective-permute-start.22 = (bf16[2,128,512]{2,1,0:T(8,128)(2,1)S(1)}, bf16[2,128,512]{2,1,0:T(8,128)(2,1)S(1)}, u32[]{:S(2)}, u32[]{:S(2)}) collective-permute-start(bf16[2,128,512]{2,1,0:T(8,128)(2,1)S(1)} %get-tuple-element.65), channel_id=1, source_target_pairs={{0,96},{1,97},{2,98},{3,99},{4,100},{5,101},{6,102},{7,103},{8,104... | collective-permute-start | bytes 786440 | tf_op jit(solution)/shard_map/ppermute | solution.py:35
  119.6 2.5 %collective-permute-start.21 = (bf16[2,128,512]{2,1,0:T(8,128)(2,1)}, bf16[2,128,512]{2,1,0:T(8,128)(2,1)S(1)}, u32[]{:S(2)}, u32[]{:S(2)}) collective-permute-start(bf16[2,128,512]{2,1,0:T(8,128)(2,1)} %slice.121), channel_id=1, source_target_pairs={{0,96},{1,97},{2,98},{3,99},{4,100},{5,101},{6,102},{7,103},{8,104... | collective-permute-start | bytes 786440 | tf_op jit(solution)/shard_map/ppermute | solution.py:35
  124.1 3.8 %collective-permute-start.23 = (bf16[2,128,512]{2,1,0:T(8,128)(2,1)S(1)}, bf16[2,128,512]{2,1,0:T(8,128)(2,1)S(1)}, u32[]{:S(2)}, u32[]{:S(2)}) collective-permute-start(bf16[2,128,512]{2,1,0:T(8,128)(2,1)S(1)} %add_convert_fusion.2), channel_id=1, source_target_pairs={{0,96},{1,97},{2,98},{3,99},{4,100},{5,101},{6,102},{7,103},{8,104... | collective-permute-start | bytes 786440 | tf_op jit(solution)/shard_map/ppermute | solution.py:35
  128.6 4.7 %collective-permute-done.20 = bf16[2,128,512]{2,1,0:T(8,128)(2,1)S(1)} collective-permute-done((bf16[2,128,512]{2,1,0:T(8,128)(2,1)}, bf16[2,128,512]{2,1,0:T(8,128)(2,1)S(1)}, u32[]{:S(2)}, u32[]{:S(2)}) %collective-permute-start.20) | collective-permute-done | bytes 262176 | tf_op jit(solution)/shard_map/ppermute | solution.py:35
  134.6 3.5 %collective-permute-done.19 = bf16[2,128,512]{2,1,0:T(8,128)(2,1)} collective-permute-done((bf16[2,128,512]{2,1,0:T(8,128)(2,1)}, bf16[2,128,512]{2,1,0:T(8,128)(2,1)}, u32[]{:S(2)}, u32[]{:S(2)}) %collective-permute-start.19) | collective-permute-done | bytes 262176 | tf_op jit(solution)/shard_map/ppermute | solution.py:35
  140.8 2.1 %collective-permute-start.25 = (bf16[256,512]{1,0:T(8,128)(2,1)S(1)}, bf16[256,512]{1,0:T(8,128)(2,1)S(1)}, u32[]{:S(2)}, u32[]{:S(2)}) collective-permute-start(bf16[256,512]{1,0:T(8,128)(2,1)S(1)} %get-tuple-element.63), channel_id=1, source_target_pairs={{0,144},{1,145},{2,146},{3,147},{4,148},{5,149},{6,150},{7,151},{8... | collective-permute-start | bytes 786440 | tf_op jit(solution)/shard_map/ppermute | solution.py:35
  142.9 3.4 %collective-permute-done.24 = bf16[256,512]{1,0:T(8,128)(2,1)S(1)} collective-permute-done((bf16[256,512]{1,0:T(8,128)(2,1)S(1)}, bf16[256,512]{1,0:T(8,128)(2,1)S(1)}, u32[]{:S(2)}, u32[]{:S(2)}) %collective-permute-start.24) | collective-permute-done | bytes 262176 | tf_op jit(solution)/shard_map/ppermute | solution.py:35
  146.4 2.4 %collective-permute-done.25 = bf16[256,512]{1,0:T(8,128)(2,1)S(1)} collective-permute-done((bf16[256,512]{1,0:T(8,128)(2,1)S(1)}, bf16[256,512]{1,0:T(8,128)(2,1)S(1)}, u32[]{:S(2)}, u32[]{:S(2)}) %collective-permute-start.25) | collective-permute-done | bytes 262176 | tf_op jit(solution)/shard_map/ppermute | solution.py:35
  148.8 2.2 %copy-done = bf16[1,1,4096,512]{3,2,1,0:T(8,128)(2,1)S(1)} copy-done((bf16[1,1,4096,512]{3,2,1,0:T(8,128)(2,1)S(1)}, bf16[1,1,4096,512]{3,2,1,0:T(8,128)(2,1)}, u32[]{:S(2)}) %copy-start) | copy-done | bytes 4194328
  151.0 2.7 %shard_map.75 = bf16[8,256,512]{2,1,0:T(8,128)(2,1)S(1)} custom-call(bf16[256,512]{1,0:T(8,128)(2,1)S(1)} %shard_map.73.refs_1_.a_ref, bf16[4096,512]{1,0:T(8,128)(2,1)S(1)} %bitcast.110), custom_call_target="tpu_custom_call" | custom-call | flops 1073741824 | bytes 6553600 | tf_op jit(solution)/shard_map/pallas_call | solution.py:186
  154.0 3.3 %collective-permute-start.28 = (bf16[2,128,512]{2,1,0:T(8,128)(2,1)S(1)}, bf16[2,128,512]{2,1,0:T(8,128)(2,1)S(1)}, u32[]{:S(2)}, u32[]{:S(2)}) collective-permute-start(bf16[2,128,512]{2,1,0:T(8,128)(2,1)S(1)} %get-tuple-element.60), channel_id=1, source_target_pairs={{0,96},{1,97},{2,98},{3,99},{4,100},{5,101},{6,102},{7,103},{8,104... | collective-permute-start | bytes 786440 | tf_op jit(solution)/shard_map/ppermute | solution.py:35
  157.3 4.2 %collective-permute-done.26 = bf16[2,128,512]{2,1,0:T(8,128)(2,1)S(1)} collective-permute-done((bf16[2,128,512]{2,1,0:T(8,128)(2,1)S(1)}, bf16[2,128,512]{2,1,0:T(8,128)(2,1)S(1)}, u32[]{:S(2)}, u32[]{:S(2)}) %collective-permute-start.26) | collective-permute-done | bytes 262176 | tf_op jit(solution)/shard_map/ppermute | solution.py:35
  161.8 3.3 %collective-permute-start.29 = (bf16[2,256,512]{2,1,0:T(8,128)(2,1)S(1)}, bf16[2,256,512]{2,1,0:T(8,128)(2,1)S(1)}, u32[]{:S(2)}, u32[]{:S(2)}) collective-permute-start(bf16[2,256,512]{2,1,0:T(8,128)(2,1)S(1)} %pad_maximum_fusion.3), channel_id=1, source_target_pairs={{0,96},{1,97},{2,98},{3,99},{4,100},{5,101},{6,102},{7,103},{8,104... | collective-permute-start | bytes 1572872 | tf_op jit(solution)/shard_map/ppermute | solution.py:35
  165.1 8.0 %collective-permute-done.27 = bf16[2,256,512]{2,1,0:T(8,128)(2,1)S(1)} collective-permute-done((bf16[2,256,512]{2,1,0:T(8,128)(2,1)S(1)}, bf16[2,256,512]{2,1,0:T(8,128)(2,1)S(1)}, u32[]{:S(2)}, u32[]{:S(2)}) %collective-permute-start.27) | collective-permute-done | bytes 524320 | tf_op jit(solution)/shard_map/ppermute | solution.py:35
  177.4 2.5 %collective-permute-done.30 = bf16[256,512]{1,0:T(8,128)(2,1)S(1)} collective-permute-done((bf16[256,512]{1,0:T(8,128)(2,1)S(1)}, bf16[256,512]{1,0:T(8,128)(2,1)S(1)}, u32[]{:S(2)}, u32[]{:S(2)}) %collective-permute-start.30) | collective-permute-done | bytes 262176 | tf_op jit(solution)/shard_map/ppermute | solution.py:35
  179.9 2.9 %collective-permute-done.31 = bf16[256,512]{1,0:T(8,128)(2,1)S(1)} collective-permute-done((bf16[256,512]{1,0:T(8,128)(2,1)S(1)}, bf16[256,512]{1,0:T(8,128)(2,1)S(1)}, u32[]{:S(2)}, u32[]{:S(2)}) %collective-permute-start.31) | collective-permute-done | bytes 262176 | tf_op jit(solution)/shard_map/ppermute | solution.py:35
  (143 shorter events, 48.2 us)
Async XLA Ops:
  6.5 93.1 %all-gather.5.cloned.1.call-start = ((), (), s32[]{:S(2)}) async-start(), calls=%async_computation | async-start | bytes 13369344 | tf_op jit(solution)/shard_map/all_gather | solution.py:248
  7.3 141.5 %all-gather.7.cloned.1.call-start = ((), (), s32[]{:S(2)}) async-start(), calls=%async_computation.1 | async-start | bytes 4456448 | tf_op jit(solution)/shard_map/all_gather | solution.py:282
  9.1 14.7 %collective-permute-start.9 = (bf16[256,512]{1,0:T(8,128)(2,1)S(1)}, bf16[256,512]{1,0:T(8,128)(2,1)S(1)}, u32[]{:S(2)}, u32[]{:S(2)}) collective-permute-start(bf16[256,512]{1,0:T(8,128)(2,1)S(1)} %get-tuple-element.32.refs_2_), channel_id=1, source_target_pairs={{0,2},{1,3},{2,4},{3,5},{4,6},{5,7},{6,8},{7,9},{8,10},{9,11},{10,... | collective-permute-start | bytes 786440 | tf_op jit(solution)/shard_map/ppermute | solution.py:35
  11.0 13.4 %collective-permute-start.8 = (bf16[256,512]{1,0:T(8,128)(2,1)S(1)}, bf16[256,512]{1,0:T(8,128)(2,1)S(1)}, u32[]{:S(2)}, u32[]{:S(2)}) collective-permute-start(bf16[256,512]{1,0:T(8,128)(2,1)S(1)} %get-tuple-element.32.refs_2_), channel_id=1, source_target_pairs={{0,14},{1,15},{2,0},{3,1},{4,2},{5,3},{6,4},{7,5},{8,6},{9,7},{10,... | collective-permute-start | bytes 786440 | tf_op jit(solution)/shard_map/ppermute | solution.py:35
  11.1 24.9 %collective-permute-start.5 = (bf16[1,4,2,1,256,128]{5,4,2,1,3,0:T(8,128)(2,1)}, bf16[1,4,2,1,256,128]{5,4,2,1,3,0:T(8,128)(2,1)}, u32[]{:S(2)}, u32[]{:S(2)}) collective-permute-start(bf16[1,4,2,1,256,128]{5,4,2,1,3,0:T(8,128)(2,1)} %bitcast.116), channel_id=1, source_target_pairs={{0,1},{1,2},{2,3},{3,4},{4,5},{5,6},{6,7},{7,8},{8,9},{9,10},{10,1... | collective-permute-start | bytes 1572872 | tf_op jit(solution)/shard_map/ppermute | solution.py:152
  11.1 29.9 %collective-permute-start.6 = (bf16[1,4,2,1,256,128]{5,4,2,1,3,0:T(8,128)(2,1)}, bf16[1,4,2,1,256,128]{5,4,2,1,3,0:T(8,128)(2,1)S(1)}, u32[]{:S(2)}, u32[]{:S(2)}) collective-permute-start(bf16[1,4,2,1,256,128]{5,4,2,1,3,0:T(8,128)(2,1)} %bitcast.117), channel_id=1, source_target_pairs={{1,0},{2,1},{3,2},{4,3},{5,4},{6,5},{7,6},{8,7},{9,8},{10,9},{11,1... | collective-permute-start | bytes 1572872 | tf_op jit(solution)/shard_map/ppermute | solution.py:153
  14.2 16.6 %collective-permute-start = (bf16[256,1024]{1,0:T(8,128)(2,1)}, bf16[256,1024]{1,0:T(8,128)(2,1)S(1)}, u32[]{:S(2)}, u32[]{:S(2)}) collective-permute-start(bf16[256,1024]{1,0:T(8,128)(2,1)} %bitcast.1), channel_id=1, source_target_pairs={{0,16},{1,17},{2,18},{3,19},{4,20},{5,21},{6,22},{7,23},{8,24},{9,... | collective-permute-start | bytes 1572872 | tf_op jit(solution)/shard_map/ppermute | solution.py:35
  23.8 64.2 %collective-permute-start.7 = (bf16[256,1024]{1,0:T(8,128)(2,1)}, bf16[256,1024]{1,0:T(8,128)(2,1)}, u32[]{:S(2)}, u32[]{:S(2)}) collective-permute-start(bf16[256,1024]{1,0:T(8,128)(2,1)} %bitcast.1), channel_id=1, source_target_pairs={{0,128},{1,129},{2,130},{3,131},{4,132},{5,133},{6,134},{7,135},{8... | collective-permute-start | bytes 1572872 | tf_op jit(solution)/shard_map/ppermute | solution.py:35
  24.5 20.0 %collective-permute-start.11 = (bf16[256,512]{1,0:T(8,128)(2,1)S(1)}, bf16[256,512]{1,0:T(8,128)(2,1)S(1)}, u32[]{:S(2)}, u32[]{:S(2)}) collective-permute-start(bf16[256,512]{1,0:T(8,128)(2,1)S(1)} %collective-permute-done.9.refs_4_), channel_id=1, source_target_pairs={{0,2},{1,3},{2,4},{3,5},{4,6},{5,7},{6,8},{7,9},{8,10},{9,11},{10,... | collective-permute-start | bytes 786440 | tf_op jit(solution)/shard_map/ppermute | solution.py:35
  30.8 14.1 %collective-permute-start.10 = (bf16[256,512]{1,0:T(8,128)(2,1)S(1)}, bf16[256,512]{1,0:T(8,128)(2,1)S(1)}, u32[]{:S(2)}, u32[]{:S(2)}) collective-permute-start(bf16[256,512]{1,0:T(8,128)(2,1)S(1)} %collective-permute-done.8.refs_3_), channel_id=1, source_target_pairs={{0,14},{1,15},{2,0},{3,1},{4,2},{5,3},{6,4},{7,5},{8,6},{9,7},{10,... | collective-permute-start | bytes 786440 | tf_op jit(solution)/shard_map/ppermute | solution.py:35
  36.0 35.5 %collective-permute-start.1 = (bf16[2,256,1024]{2,1,0:T(8,128)(2,1)}, bf16[2,256,1024]{2,1,0:T(8,128)(2,1)}, u32[]{:S(2)}, u32[]{:S(2)}) collective-permute-start(bf16[2,256,1024]{2,1,0:T(8,128)(2,1)} %pad_maximum_fusion), channel_id=1, source_target_pairs={{0,96},{1,97},{2,98},{3,99},{4,100},{5,101},{6,102},{7,103},{8,104... | collective-permute-start | bytes 3145736 | tf_op jit(solution)/shard_map/ppermute | solution.py:35
  41.1 28.8 %collective-permute-start.2 = (bf16[2,256,1024]{2,1,0:T(8,128)(2,1)}, bf16[2,256,1024]{2,1,0:T(8,128)(2,1)}, u32[]{:S(2)}, u32[]{:S(2)}) collective-permute-start(bf16[2,256,1024]{2,1,0:T(8,128)(2,1)} %pad_maximum_fusion), channel_id=1, source_target_pairs={{0,32},{1,33},{2,34},{3,35},{4,36},{5,37},{6,38},{7,39},{8,40},{9,... | collective-permute-start | bytes 3145736 | tf_op jit(solution)/shard_map/ppermute | solution.py:35
  44.5 13.5 %collective-permute-start.13 = (bf16[256,512]{1,0:T(8,128)(2,1)S(1)}, bf16[256,512]{1,0:T(8,128)(2,1)S(1)}, u32[]{:S(2)}, u32[]{:S(2)}) collective-permute-start(bf16[256,512]{1,0:T(8,128)(2,1)S(1)} %collective-permute-done.11.refs_6_), channel_id=1, source_target_pairs={{0,2},{1,3},{2,4},{3,5},{4,6},{5,7},{6,8},{7,9},{8,10},{9,11},{10,... | collective-permute-start | bytes 786440 | tf_op jit(solution)/shard_map/ppermute | solution.py:35
  44.9 14.6 %collective-permute-start.12 = (bf16[256,512]{1,0:T(8,128)(2,1)S(1)}, bf16[256,512]{1,0:T(8,128)(2,1)S(1)}, u32[]{:S(2)}, u32[]{:S(2)}) collective-permute-start(bf16[256,512]{1,0:T(8,128)(2,1)S(1)} %collective-permute-done.10.refs_5_), channel_id=1, source_target_pairs={{0,14},{1,15},{2,0},{3,1},{4,2},{5,3},{6,4},{7,5},{8,6},{9,7},{10,... | collective-permute-start | bytes 786440 | tf_op jit(solution)/shard_map/ppermute | solution.py:35
  58.0 8.6 %collective-permute-start.14 = (bf16[128,512]{1,0:T(8,128)(2,1)S(1)}, bf16[128,512]{1,0:T(8,128)(2,1)S(1)}, u32[]{:S(2)}, u32[]{:S(2)}) collective-permute-start(bf16[128,512]{1,0:T(8,128)(2,1)S(1)} %slice.116), channel_id=1, source_target_pairs={{0,2},{1,3},{2,4},{3,5},{4,6},{5,7},{6,8},{7,9},{8,10},{9,11},{10,... | collective-permute-start | bytes 393224 | tf_op jit(solution)/shard_map/ppermute | solution.py:35
  59.4 29.5 %collective-permute-start.16 = (bf16[5,256,512]{2,1,0:T(8,128)(2,1)S(1)}, bf16[5,256,512]{2,1,0:T(8,128)(2,1)S(1)}, u32[]{:S(2)}, u32[]{:S(2)}) collective-permute-start(bf16[5,256,512]{2,1,0:T(8,128)(2,1)S(1)} %bitcast_dynamic-update-slice_fusion.10), channel_id=1, source_target_pairs={{0,1},{1,0},{2,3},{3,2},{4,5},{5,4},{6,7},{7,6},{8,9},{9,8},{10,11... | collective-permute-start | bytes 3932168 | tf_op jit(solution)/shard_map/ppermute | solution.py:35
  66.6 8.8 %collective-permute-start.15 = (bf16[128,512]{1,0:T(8,128)(2,1)S(1)}, bf16[128,512]{1,0:T(8,128)(2,1)S(1)}, u32[]{:S(2)}, u32[]{:S(2)}) collective-permute-start(bf16[128,512]{1,0:T(8,128)(2,1)S(1)} %slice.117), channel_id=1, source_target_pairs={{0,14},{1,15},{2,0},{3,1},{4,2},{5,3},{6,4},{7,5},{8,6},{9,7},{10,... | collective-permute-start | bytes 393224 | tf_op jit(solution)/shard_map/ppermute | solution.py:35
  70.9 10.5 %collective-permute-start.3 = (bf16[256,1024]{1,0:T(8,128)(2,1)S(1)}, bf16[256,1024]{1,0:T(8,128)(2,1)S(1)}, u32[]{:S(2)}, u32[]{:S(2)}) collective-permute-start(bf16[256,1024]{1,0:T(8,128)(2,1)S(1)} %slice_bitcast_fusion.1), channel_id=1, source_target_pairs={{0,32},{1,33},{2,34},{3,35},{4,36},{5,37},{6,38},{7,39},{8,40},{9,... | collective-permute-start | bytes 1572872 | tf_op jit(solution)/shard_map/ppermute | solution.py:35
  72.6 9.5 %collective-permute-start.4 = (bf16[256,1024]{1,0:T(8,128)(2,1)S(1)}, bf16[256,1024]{1,0:T(8,128)(2,1)S(1)}, u32[]{:S(2)}, u32[]{:S(2)}) collective-permute-start(bf16[256,1024]{1,0:T(8,128)(2,1)S(1)} %slice_bitcast_fusion), channel_id=1, source_target_pairs={{0,96},{1,97},{2,98},{3,99},{4,100},{5,101},{6,102},{7,103},{8,104... | collective-permute-start | bytes 1572872 | tf_op jit(solution)/shard_map/ppermute | solution.py:35
  75.5 12.5 %collective-permute-start.17 = (bf16[3,256,512]{2,1,0:T(8,128)(2,1)S(1)}, bf16[3,256,512]{2,1,0:T(8,128)(2,1)S(1)}, u32[]{:S(2)}, u32[]{:S(2)}) collective-permute-start(bf16[3,256,512]{2,1,0:T(8,128)(2,1)S(1)} %pad_maximum_fusion.1), channel_id=1, source_target_pairs={{0,1},{1,0},{2,3},{3,2},{4,5},{5,4},{6,7},{7,6},{8,9},{9,8},{10,11... | collective-permute-start | bytes 2359304 | tf_op jit(solution)/shard_map/ppermute | solution.py:35
  114.5 9.5 %collective-permute-start.22 = (bf16[2,128,512]{2,1,0:T(8,128)(2,1)S(1)}, bf16[2,128,512]{2,1,0:T(8,128)(2,1)S(1)}, u32[]{:S(2)}, u32[]{:S(2)}) collective-permute-start(bf16[2,128,512]{2,1,0:T(8,128)(2,1)S(1)} %get-tuple-element.65), channel_id=1, source_target_pairs={{0,96},{1,97},{2,98},{3,99},{4,100},{5,101},{6,102},{7,103},{8,104... | collective-permute-start | bytes 786440 | tf_op jit(solution)/shard_map/ppermute | solution.py:35
  117.4 10.5 %collective-permute-start.18 = (bf16[2,128,512]{2,1,0:T(8,128)(2,1)S(1)}, bf16[2,128,512]{2,1,0:T(8,128)(2,1)S(1)}, u32[]{:S(2)}, u32[]{:S(2)}) collective-permute-start(bf16[2,128,512]{2,1,0:T(8,128)(2,1)S(1)} %get-tuple-element.66), channel_id=1, source_target_pairs={{0,32},{1,33},{2,34},{3,35},{4,36},{5,37},{6,38},{7,39},{8,40},{9,... | collective-permute-start | bytes 786440 | tf_op jit(solution)/shard_map/ppermute | solution.py:35
  118.1 15.3 %collective-permute-start.20 = (bf16[2,128,512]{2,1,0:T(8,128)(2,1)}, bf16[2,128,512]{2,1,0:T(8,128)(2,1)S(1)}, u32[]{:S(2)}, u32[]{:S(2)}) collective-permute-start(bf16[2,128,512]{2,1,0:T(8,128)(2,1)} %slice.120), channel_id=1, source_target_pairs={{0,32},{1,33},{2,34},{3,35},{4,36},{5,37},{6,38},{7,39},{8,40},{9,... | collective-permute-start | bytes 786440 | tf_op jit(solution)/shard_map/ppermute | solution.py:35
  119.6 13.8 %collective-permute-start.21 = (bf16[2,128,512]{2,1,0:T(8,128)(2,1)}, bf16[2,128,512]{2,1,0:T(8,128)(2,1)S(1)}, u32[]{:S(2)}, u32[]{:S(2)}) collective-permute-start(bf16[2,128,512]{2,1,0:T(8,128)(2,1)} %slice.121), channel_id=1, source_target_pairs={{0,96},{1,97},{2,98},{3,99},{4,100},{5,101},{6,102},{7,103},{8,104... | collective-permute-start | bytes 786440 | tf_op jit(solution)/shard_map/ppermute | solution.py:35
  124.1 10.5 %collective-permute-start.23 = (bf16[2,128,512]{2,1,0:T(8,128)(2,1)S(1)}, bf16[2,128,512]{2,1,0:T(8,128)(2,1)S(1)}, u32[]{:S(2)}, u32[]{:S(2)}) collective-permute-start(bf16[2,128,512]{2,1,0:T(8,128)(2,1)S(1)} %add_convert_fusion.2), channel_id=1, source_target_pairs={{0,96},{1,97},{2,98},{3,99},{4,100},{5,101},{6,102},{7,103},{8,104... | collective-permute-start | bytes 786440 | tf_op jit(solution)/shard_map/ppermute | solution.py:35
  128.6 9.4 %collective-permute-start.19 = (bf16[2,128,512]{2,1,0:T(8,128)(2,1)}, bf16[2,128,512]{2,1,0:T(8,128)(2,1)}, u32[]{:S(2)}, u32[]{:S(2)}) collective-permute-start(bf16[2,128,512]{2,1,0:T(8,128)(2,1)} %add_convert_fusion.3), channel_id=1, source_target_pairs={{0,32},{1,33},{2,34},{3,35},{4,36},{5,37},{6,38},{7,39},{8,40},{9,... | collective-permute-start | bytes 786440 | tf_op jit(solution)/shard_map/ppermute | solution.py:35
  140.8 7.9 %collective-permute-start.25 = (bf16[256,512]{1,0:T(8,128)(2,1)S(1)}, bf16[256,512]{1,0:T(8,128)(2,1)S(1)}, u32[]{:S(2)}, u32[]{:S(2)}) collective-permute-start(bf16[256,512]{1,0:T(8,128)(2,1)S(1)} %get-tuple-element.63), channel_id=1, source_target_pairs={{0,144},{1,145},{2,146},{3,147},{4,148},{5,149},{6,150},{7,151},{8... | collective-permute-start | bytes 786440 | tf_op jit(solution)/shard_map/ppermute | solution.py:35
  153.9 7.7 %collective-permute-start.26 = (bf16[2,128,512]{2,1,0:T(8,128)(2,1)S(1)}, bf16[2,128,512]{2,1,0:T(8,128)(2,1)S(1)}, u32[]{:S(2)}, u32[]{:S(2)}) collective-permute-start(bf16[2,128,512]{2,1,0:T(8,128)(2,1)S(1)} %get-tuple-element.59), channel_id=1, source_target_pairs={{0,32},{1,33},{2,34},{3,35},{4,36},{5,37},{6,38},{7,39},{8,40},{9,... | collective-permute-start | bytes 786440 | tf_op jit(solution)/shard_map/ppermute | solution.py:35
  154.0 7.7 %collective-permute-start.28 = (bf16[2,128,512]{2,1,0:T(8,128)(2,1)S(1)}, bf16[2,128,512]{2,1,0:T(8,128)(2,1)S(1)}, u32[]{:S(2)}, u32[]{:S(2)}) collective-permute-start(bf16[2,128,512]{2,1,0:T(8,128)(2,1)S(1)} %get-tuple-element.60), channel_id=1, source_target_pairs={{0,96},{1,97},{2,98},{3,99},{4,100},{5,101},{6,102},{7,103},{8,104... | collective-permute-start | bytes 786440 | tf_op jit(solution)/shard_map/ppermute | solution.py:35
  161.6 11.5 %collective-permute-start.27 = (bf16[2,256,512]{2,1,0:T(8,128)(2,1)S(1)}, bf16[2,256,512]{2,1,0:T(8,128)(2,1)S(1)}, u32[]{:S(2)}, u32[]{:S(2)}) collective-permute-start(bf16[2,256,512]{2,1,0:T(8,128)(2,1)S(1)} %pad_maximum_fusion.2), channel_id=1, source_target_pairs={{0,32},{1,33},{2,34},{3,35},{4,36},{5,37},{6,38},{7,39},{8,40},{9,... | collective-permute-start | bytes 1572872 | tf_op jit(solution)/shard_map/ppermute | solution.py:35
  161.8 11.3 %collective-permute-start.29 = (bf16[2,256,512]{2,1,0:T(8,128)(2,1)S(1)}, bf16[2,256,512]{2,1,0:T(8,128)(2,1)S(1)}, u32[]{:S(2)}, u32[]{:S(2)}) collective-permute-start(bf16[2,256,512]{2,1,0:T(8,128)(2,1)S(1)} %pad_maximum_fusion.3), channel_id=1, source_target_pairs={{0,96},{1,97},{2,98},{3,99},{4,100},{5,101},{6,102},{7,103},{8,104... | collective-permute-start | bytes 1572872 | tf_op jit(solution)/shard_map/ppermute | solution.py:35
  175.2 7.6 %collective-permute-start.31 = (bf16[256,512]{1,0:T(8,128)(2,1)S(1)}, bf16[256,512]{1,0:T(8,128)(2,1)S(1)}, u32[]{:S(2)}, u32[]{:S(2)}) collective-permute-start(bf16[256,512]{1,0:T(8,128)(2,1)S(1)} %get-tuple-element.57), channel_id=1, source_target_pairs={{0,144},{1,145},{2,146},{3,147},{4,148},{5,149},{6,150},{7,151},{8... | collective-permute-start | bytes 786440 | tf_op jit(solution)/shard_map/ppermute | solution.py:35
  (19 other events, 191.0 us)
Sparse Core Ops, SparseCore 0:
  9.2 90.4 all-gather.4
  101.5 43.7 all-gather.6

commit v3 on v2

--- a/solution.py
+++ b/solution.py
@@ -13,6 +13,7 @@
 
 AXES = ("segment", "tensor", "particle")
 SEG, NY, NXH, NZ, NC = 2, 4, 2, 8, 2
+WIDE = 256
 SCOPE = pltpu.CompilerParams(vmem_limit_bytes=40 * 2**20)
 
 
@@ -204,17 +205,19 @@
 def ring_terms_kernel(order, place_ref, a_ref, *refs):
     own, partners, o_ref = refs[: len(order)], refs[len(order) : -1], refs[-1]
     z, c = place_ref[0], place_ref[1]
-    rows = own[0].shape[0]
     a = a_ref[...]
-    at = 0
-    for k, block in zip(order, own):
+    others = [group.at[g] for group in partners for g in range(group.shape[0])]
+    for k, block, other in zip(order, own, others):
         to = lax.rem(z + k, NZ)
-        o_ref[to, :, pl.ds(pl.multiple_of(c * rows, rows), rows)] = term(a, block[...])
-    for group in partners:
-        for g in range(group.shape[0]):
-            to = lax.rem(z + order[at], NZ)
-            o_ref[to, :, pl.ds(pl.multiple_of((1 - c) * rows, rows), rows)] = term(a, group[g])
-            at += 1
+        mine, theirs = term(a, block[...]), term(a, other[...])
+        o_ref[to, :, pl.ds(pl.multiple_of(c * WIDE, WIDE), WIDE)] = mine[:, :WIDE]
+        o_ref[to, :, pl.ds(pl.multiple_of((1 - c) * WIDE, WIDE), WIDE)] = theirs[:, :WIDE]
+        mine, theirs = mine[:, WIDE:], theirs[:, WIDE:]
+        o_ref[to, :, NC * WIDE :] = jnp.where(
+            c == 0,
+            jnp.concatenate([mine, theirs], axis=1),
+            jnp.concatenate([theirs, mine], axis=1),
+        )
 
 
 def ring_terms(a, order, own, partners, place):
@@ -243,7 +246,7 @@
     x0 = step_states[0]
     tokens, features = x0.shape
     shards = NY * NXH
-    rows = w_out.shape[2] // 2
+    cut = w_out.shape[2] * 5 // 8
 
     w_full = lax.all_gather(w_qkv[0, 0], "particle", axis=0, tiled=True)
 
@@ -269,7 +272,7 @@
     hidden = send(x0, ds=1)
     picked, lengths = picked_cache(prefix_cache, ancestors, prefix_lengths)
 
-    around = ring(w_out[0, 0, :rows])
+    around = ring(w_out[0, 0, :cut])
     order = (0, 1, 7, 2, 6, 3, 5, 4)
     own = [around[k] for k in order]
     partners = [send(jnp.stack(own[:5]), dc=1), send(jnp.stack(own[5:]), dc=1)]
@@ -279,7 +282,7 @@
     w_full, normed, cache, cosine_part, sine_part, hidden, own, partners = lax.optimization_barrier(
         (w_full, normed, cache, cosine_part, sine_part, hidden, own, partners)
     )
-    second = lax.all_gather(w_out[0, 0, rows:], "particle", axis=0, tiled=True)
+    second = lax.all_gather(w_out[0, 0, cut:], "particle", axis=0, tiled=True)
     projected = jnp.dot(normed, w_full, preferred_element_type=jnp.float32)
     attended = attend(projected, cosine_part, sine_part, cache, lengths, group_heads)
 
@@ -289,7 +292,7 @@
             terms = ring_terms(attended, order, own, partners, jnp.stack([z, c]))
         else:
             terms = head_terms(attended, second)
-        terms = terms.reshape(NY, NXH, tokens, NC * rows)
+        terms = terms.reshape((NY, NXH) + terms.shape[1:])
         mid = tokens // 2
 
         def low_high(dy):
@@ -317,13 +320,20 @@
             + from_below.astype(jnp.float32)
             + from_above.astype(jnp.float32)
         ).astype(jnp.bfloat16)
+        attended, summed = lax.optimization_barrier((attended, summed))
         same = send(jnp.where(xh == 0, summed[0], summed[1]), ds=1)
         cross = send(jnp.where(xh == 0, summed[1], summed[0]), ds=1, dxh=1)
-        attended, same, cross = lax.optimization_barrier((attended, same, cross))
         results.append(same.astype(jnp.float32) + cross.astype(jnp.float32))
-    summed = jnp.concatenate(
-        [r[:, k * rows : (k + 1) * rows] for k in range(NC) for r in results], axis=1
-    )
+    early, late = results
+    spare, tail = cut - WIDE, late.shape[1] // NC
+    parts = []
+    for k in range(NC):
+        parts += [
+            early[:, k * WIDE : (k + 1) * WIDE],
+            early[:, NC * WIDE + k * spare : NC * WIDE + (k + 1) * spare],
+            late[:, k * tail : (k + 1) * tail],
+        ]
+    summed = jnp.concatenate(parts, axis=1)
     return (hidden.astype(jnp.float32) + summed).astype(jnp.bfloat16)[None]
 
 

time: 194 us -> 193 us (level)
  waiting for transfers between devices: 75.4 us -> 70.5 us
  local copies, waits for them, and re-layouts: 21.9 us -> 24 us
    all_gather x1, waiting for transfers between devices: 10.7 us -> 6.78 us  [body(): w_full = lax.all_gather(w_qkv[0, 0], 'particle', axis=0, tiled=True)]
    unnamed x52 -> x66, local copies, waits for them, and re-layouts: 11.4 us -> 11.3 us
  transfers between devices with their start and end apart: 34 -> 34, of which waited for: 18 -> 20; matrix products, arithmetic and copies ran while one was open for 21% -> 22% of each run, Pallas kernels for 2% -> 3%
where the time goes in v3:
time: 193 us; the launch traced here: 190 us
  waiting for transfers between devices  70.5 us (37%)
  starting transfers between devices  47.8 us (25%)
  local copies, waits for them, and re-layouts  24 us (12%)
  other arithmetic  14.3 us (7%)
  between operations  14.1 us (7%)
  matrix products  11.5 us (6%)
  Pallas kernels  8.06 us (4%)
    ppermute x30, waiting for transfers between devices, send(): return lax.ppermute(value, AXES, moves(**shift))  63 us
    ppermute x30, starting transfers between devices, send(): return lax.ppermute(value, AXES, moves(**shift))  44.6 us
    unnamed x66, local copies, waits for them, and re-layouts  11.3 us
    dot_general x1, matrix products, body(): projected = jnp.dot(normed, w_full, preferred_element_type=jnp.float32)  8.98 us
    all_gather x1, waiting for transfers between devices, body(): w_full = lax.all_gather(w_qkv[0, 0], 'particle', axis=0, tiled=True)  6.78 us
    concatenate x3, local copies, waits for them, and re-layouts, picked_cache(): extended = jnp.concatenate([before, caches, after], axis=1)  5.05 us
  transfers between devices with their start and end apart: 34, of which 20 were waited for; matrix products, arithmetic and copies ran while one was open for 22% of the time, Pallas kernels for 3%

profile of v3, /device:TPU:32, one launch (start us, length us, event | category | flops | bytes accessed | tf_op | source)
XLA Modules:
  0.0 190.3 jit_solution(165860268929725451)
XLA Ops:
  10.4 3.2 %collective-permute-start.6 = (bf16[1,4,2,1,256,128]{5,4,2,1,3,0:T(8,128)(2,1)}, bf16[1,4,2,1,256,128]{5,4,2,1,3,0:T(8,128)(2,1)}, u32[]{:S(2)}, u32[]{:S(2)}) collective-permute-start(bf16[1,4,2,1,256,128]{5,4,2,1,3,0:T(8,128)(2,1)} %bitcast.117), channel_id=1, source_target_pairs={{1,0},{2,1},{3,2},{4,3},{5,4},{6,5},{7,6},{8,7},{9,8},{10,9},{11,1... | collective-permute-start | bytes 1572872 | tf_op jit(solution)/shard_map/ppermute | solution.py:154
  13.6 3.0 %collective-permute-start = (bf16[256,1024]{1,0:T(8,128)(2,1)}, bf16[256,1024]{1,0:T(8,128)(2,1)S(1)}, u32[]{:S(2)}, u32[]{:S(2)}) collective-permute-start(bf16[256,1024]{1,0:T(8,128)(2,1)} %bitcast.1), channel_id=1, source_target_pairs={{0,16},{1,17},{2,18},{3,19},{4,20},{5,21},{6,22},{7,23},{8,24},{9,... | collective-permute-start | bytes 1572872 | tf_op jit(solution)/shard_map/ppermute | solution.py:36
  29.2 2.5 %collective-permute-start.10 = (bf16[320,512]{1,0:T(8,128)(2,1)S(1)}, bf16[320,512]{1,0:T(8,128)(2,1)S(1)}, u32[]{:S(2)}, u32[]{:S(2)}) collective-permute-start(bf16[320,512]{1,0:T(8,128)(2,1)S(1)} %collective-permute-done.8.refs_3_), channel_id=1, source_target_pairs={{0,14},{1,15},{2,0},{3,1},{4,2},{5,3},{6,4},{7,5},{8,6},{9,7},{10,... | collective-permute-start | bytes 983048 | tf_op jit(solution)/shard_map/ppermute | solution.py:36
  31.7 2.1 %pad_maximum_fusion = bf16[2,256,1024]{2,1,0:T(8,128)(2,1)} fusion(bf16[1,256,1024]{2,1,0:T(8,128)(2,1)S(1)} %bitcast.115, bf16[1,256,1024]{2,1,0:T(8,128)(2,1)} %param.7), kind=kLoop, calls=%fused_computation.15 | loop fusion | flops 524288 | bytes 2097152 | tf_op jit(solution)/shard_map/stack | solution.py:253
  33.9 3.0 %collective-permute-start.1 = (bf16[2,256,1024]{2,1,0:T(8,128)(2,1)}, bf16[2,256,1024]{2,1,0:T(8,128)(2,1)}, u32[]{:S(2)}, u32[]{:S(2)}) collective-permute-start(bf16[2,256,1024]{2,1,0:T(8,128)(2,1)} %pad_maximum_fusion), channel_id=1, source_target_pairs={{0,96},{1,97},{2,98},{3,99},{4,100},{5,101},{6,102},{7,103},{8,104... | collective-permute-start | bytes 3145736 | tf_op jit(solution)/shard_map/ppermute | solution.py:36
  41.0 2.5 %fusion.9 = bf16[1,4,512,128]{3,1,2,0:T(4,128)(2,1)S(1)} fusion(bf16[1,4,65536]{2,1,0:T(4,128)(2,1)} %concatenate.47, bf16[1,4,65536]{2,1,0:T(4,128)(2,1)S(1)} %copy-done.20, bf16[1,4,65536]{2,1,0:T(4,128)(2,1)} %concatenate.45, s32[4]{0:T(128)S(1)} %fusion.15), kind=kOutput, calls=%fused_computation.14 | convolution fusion | flops 11272240 | bytes 2097168 | tf_op jit(solution)/shard_map/jk,lkr->ljr/dot_general | solution.py:129
  44.6 2.2 %collective-permute-done.10.refs_5_ = bf16[320,512]{1,0:T(8,128)(2,1)S(1)} collective-permute-done((bf16[320,512]{1,0:T(8,128)(2,1)S(1)}, bf16[320,512]{1,0:T(8,128)(2,1)S(1)}, u32[]{:S(2)}, u32[]{:S(2)}) %collective-permute-start.10) | collective-permute-done | bytes 327712 | tf_op jit(solution)/shard_map/ppermute | solution.py:36
  46.7 2.1 %collective-permute-start.12 = (bf16[320,512]{1,0:T(8,128)(2,1)S(1)}, bf16[320,512]{1,0:T(8,128)(2,1)S(1)}, u32[]{:S(2)}, u32[]{:S(2)}) collective-permute-start(bf16[320,512]{1,0:T(8,128)(2,1)S(1)} %collective-permute-done.10.refs_5_), channel_id=1, source_target_pairs={{0,14},{1,15},{2,0},{3,1},{4,2},{5,3},{6,4},{7,5},{8,6},{9,7},{10,... | collective-permute-start | bytes 983048 | tf_op jit(solution)/shard_map/ppermute | solution.py:36
  49.0 12.4 %collective-permute-done.13.refs_8_ = bf16[320,512]{1,0:T(8,128)(2,1)S(1)} collective-permute-done((bf16[320,512]{1,0:T(8,128)(2,1)S(1)}, bf16[320,512]{1,0:T(8,128)(2,1)S(1)}, u32[]{:S(2)}, u32[]{:S(2)}) %collective-permute-start.13) | collective-permute-done | bytes 327712 | tf_op jit(solution)/shard_map/ppermute | solution.py:36
  62.6 2.4 %collective-permute-done.12.refs_7_ = bf16[320,512]{1,0:T(8,128)(2,1)S(1)} collective-permute-done((bf16[320,512]{1,0:T(8,128)(2,1)S(1)}, bf16[320,512]{1,0:T(8,128)(2,1)S(1)}, u32[]{:S(2)}, u32[]{:S(2)}) %collective-permute-start.12) | collective-permute-done | bytes 327712 | tf_op jit(solution)/shard_map/ppermute | solution.py:36
  66.6 5.2 %collective-permute-done.14 = bf16[160,512]{1,0:T(8,128)(2,1)S(1)} collective-permute-done((bf16[160,512]{1,0:T(8,128)(2,1)S(1)}, bf16[160,512]{1,0:T(8,128)(2,1)S(1)}, u32[]{:S(2)}, u32[]{:S(2)}) %collective-permute-start.14) | collective-permute-done | bytes 163872 | tf_op jit(solution)/shard_map/ppermute | solution.py:36
  71.8 3.5 %collective-permute-done.15 = bf16[160,512]{1,0:T(8,128)(2,1)S(1)} collective-permute-done((bf16[160,512]{1,0:T(8,128)(2,1)S(1)}, bf16[160,512]{1,0:T(8,128)(2,1)S(1)}, u32[]{:S(2)}, u32[]{:S(2)}) %collective-permute-start.15) | collective-permute-done | bytes 163872 | tf_op jit(solution)/shard_map/ppermute | solution.py:36
  82.5 6.1 %collective-permute-done.3 = bf16[256,1024]{1,0:T(8,128)(2,1)S(1)} collective-permute-done((bf16[256,1024]{1,0:T(8,128)(2,1)S(1)}, bf16[256,1024]{1,0:T(8,128)(2,1)S(1)}, u32[]{:S(2)}, u32[]{:S(2)}) %collective-permute-start.3) | collective-permute-done | bytes 524320 | tf_op jit(solution)/shard_map/ppermute | solution.py:36
  92.6 3.1 %fusion.2 = bf16[256,8192]{1,0:T(8,128)(2,1)} fusion(bf16[256,8192]{1,0:T(8,128)(2,1)S(1)} %bitcast_dynamic-update-slice_fusion, f32[8192]{0:T(1024)S(1)} %bitcast.118, f32[256]{0:T(256)S(1)} %add_rsqrt_fusion), kind=kLoop, calls=%fused_computation.5 | loop fusion | flops 8388608 | bytes 8422400 | tf_op jit(solution)/shard_map/convert_element_type | solution.py:270
  96.7 6.8 %all-gather.5.cloned.1.call-done = bf16[1,1,8192,768]{3,2,1,0:T(8,128)(2,1)} async-done(((bf16[1,1,512,768]{3,2,1,0:T(8,128)(2,1)}), bf16[1,1,8192,768]{3,2,1,0:T(8,128)(2,1)}) %all-gather.5.cloned.1.call-update) | async-done | bytes 12582928 | tf_op jit(solution)/shard_map/all_gather | solution.py:251
  103.5 9.0 %fusion.25.refs_1_ = f32[256,768]{1,0:T(8,128)S(1)} fusion(bf16[256,8192]{1,0:T(8,128)(2,1)} %fusion.2, bf16[8192,768]{1,0:T(8,128)(2,1)} %bitcast.119), kind=kOutput, calls=%fused_computation.97 | convolution fusion | flops 3221225472 | bytes 17563648 | tf_op jit(solution)/shard_map/dot_general | solution.py:286
  112.5 2.4 %shard_map.73.refs_1_.a_ref = bf16[256,512]{1,0:T(8,128)(2,1)S(1)} custom-call(s32[4]{0:T(128)S(1)} %select_reduce_fusion.refs_0_, f32[256,768]{1,0:T(8,128)S(1)} %fusion.25.refs_1_, f32[256,128]{1,0:T(8,128)S(1)} %get-tuple-element.27.refs_2_, f32[256,128]{1,0:T(8,128)S(1)} %copy-done.17, bf16[4,2,256,128]{3,2,1,0:T(8,128)(2,1)S(1)} %bitcast.111), custom_call_target="tpu_custom_call" | custom-call | flops 167772160 | bytes 1310720 | tf_op jit(solution)/shard_map/pallas_call | solution.py:109
  116.5 3.0 %shard_map.74 = bf16[8,256,640]{2,1,0:T(8,128)(2,1)S(1)} custom-call(s32[2]{0:T(128)S(1)} %pad_add_fusion.refs_0_, bf16[256,512]{1,0:T(8,128)(2,1)S(1)} %shard_map.73.refs_1_.a_ref, bf16[320,512]{1,0:T(8,128)(2,1)S(1)} %copy-done.6, bf16[320,512]{1,0:T(8,128)(2,1)S(1)} %copy-done.10, bf16[320,512]{1,0:T(8,128)(2,1)S(1)} %copy-done.8, ...), custom_call_target="tpu_custom_call" | custom-call | flops 1342177280 | bytes 8126464 | tf_op jit(solution)/shard_map/pallas_call | solution.py:226
  119.7 3.1 %collective-permute-start.22 = (bf16[2,128,640]{2,1,0:T(8,128)(2,1)S(1)}, bf16[2,128,640]{2,1,0:T(8,128)(2,1)S(1)}, u32[]{:S(2)}, u32[]{:S(2)}) collective-permute-start(bf16[2,128,640]{2,1,0:T(8,128)(2,1)S(1)} %get-tuple-element.55), channel_id=1, source_target_pairs={{0,96},{1,97},{2,98},{3,99},{4,100},{5,101},{6,102},{7,103},{8,104... | collective-permute-start | bytes 983048 | tf_op jit(solution)/shard_map/ppermute | solution.py:36
  123.6 2.7 %collective-permute-start.21 = (bf16[2,128,640]{2,1,0:T(8,128)(2,1)S(1)}, bf16[2,128,640]{2,1,0:T(8,128)(2,1)}, u32[]{:S(2)}, u32[]{:S(2)}) collective-permute-start(bf16[2,128,640]{2,1,0:T(8,128)(2,1)S(1)} %slice.129), channel_id=1, source_target_pairs={{0,96},{1,97},{2,98},{3,99},{4,100},{5,101},{6,102},{7,103},{8,104... | collective-permute-start | bytes 983048 | tf_op jit(solution)/shard_map/ppermute | solution.py:36
  126.3 4.6 %collective-permute-done.22 = bf16[2,128,640]{2,1,0:T(8,128)(2,1)S(1)} collective-permute-done((bf16[2,128,640]{2,1,0:T(8,128)(2,1)S(1)}, bf16[2,128,640]{2,1,0:T(8,128)(2,1)S(1)}, u32[]{:S(2)}, u32[]{:S(2)}) %collective-permute-start.22) | collective-permute-done | bytes 327712 | tf_op jit(solution)/shard_map/ppermute | solution.py:36
  131.7 3.7 %collective-permute-start.23 = (bf16[2,128,640]{2,1,0:T(8,128)(2,1)}, bf16[2,128,640]{2,1,0:T(8,128)(2,1)}, u32[]{:S(2)}, u32[]{:S(2)}) collective-permute-start(bf16[2,128,640]{2,1,0:T(8,128)(2,1)} %add_convert_fusion.1), channel_id=1, source_target_pairs={{0,96},{1,97},{2,98},{3,99},{4,100},{5,101},{6,102},{7,103},{8,104... | collective-permute-start | bytes 983048 | tf_op jit(solution)/shard_map/ppermute | solution.py:36
  136.2 5.5 %collective-permute-done.20 = bf16[2,128,640]{2,1,0:T(8,128)(2,1)} collective-permute-done((bf16[2,128,640]{2,1,0:T(8,128)(2,1)S(1)}, bf16[2,128,640]{2,1,0:T(8,128)(2,1)}, u32[]{:S(2)}, u32[]{:S(2)}) %collective-permute-start.20) | collective-permute-done | bytes 327712 | tf_op jit(solution)/shard_map/ppermute | solution.py:36
  141.8 2.6 %collective-permute-done.23 = bf16[2,128,640]{2,1,0:T(8,128)(2,1)} collective-permute-done((bf16[2,128,640]{2,1,0:T(8,128)(2,1)}, bf16[2,128,640]{2,1,0:T(8,128)(2,1)}, u32[]{:S(2)}, u32[]{:S(2)}) %collective-permute-start.23) | collective-permute-done | bytes 327712 | tf_op jit(solution)/shard_map/ppermute | solution.py:36
  144.3 3.4 %collective-permute-done.19 = bf16[2,128,640]{2,1,0:T(8,128)(2,1)} collective-permute-done((bf16[2,128,640]{2,1,0:T(8,128)(2,1)}, bf16[2,128,640]{2,1,0:T(8,128)(2,1)}, u32[]{:S(2)}, u32[]{:S(2)}) %collective-permute-start.19) | collective-permute-done | bytes 327712 | tf_op jit(solution)/shard_map/ppermute | solution.py:36
  151.2 2.6 %shard_map.75 = bf16[8,256,384]{2,1,0:T(8,128)(2,1)S(1)} custom-call(bf16[256,512]{1,0:T(8,128)(2,1)S(1)} %shard_map.73.refs_1_.a_ref, bf16[3072,512]{1,0:T(8,128)(2,1)S(1)} %bitcast.110), custom_call_target="tpu_custom_call" | custom-call | flops 805306368 | bytes 4980736 | tf_op jit(solution)/shard_map/pallas_call | solution.py:187
  154.6 2.8 %collective-permute-start.28 = (bf16[2,128,384]{2,1,0:T(8,128)(2,1)S(1)}, bf16[2,128,384]{2,1,0:T(8,128)(2,1)S(1)}, u32[]{:S(2)}, u32[]{:S(2)}) collective-permute-start(bf16[2,128,384]{2,1,0:T(8,128)(2,1)S(1)} %get-tuple-element.62), channel_id=1, source_target_pairs={{0,96},{1,97},{2,98},{3,99},{4,100},{5,101},{6,102},{7,103},{8,104... | collective-permute-start | bytes 589832 | tf_op jit(solution)/shard_map/ppermute | solution.py:36
  159.1 2.1 %collective-permute-start.25 = (bf16[256,640]{1,0:T(8,128)(2,1)S(1)}, bf16[256,640]{1,0:T(8,128)(2,1)S(1)}, u32[]{:S(2)}, u32[]{:S(2)}) collective-permute-start(bf16[256,640]{1,0:T(8,128)(2,1)S(1)} %get-tuple-element.54), channel_id=1, source_target_pairs={{0,144},{1,145},{2,146},{3,147},{4,148},{5,149},{6,150},{7,151},{8... | collective-permute-start | bytes 983048 | tf_op jit(solution)/shard_map/ppermute | solution.py:36
  161.9 3.0 %collective-permute-start.29 = (bf16[2,256,384]{2,1,0:T(8,128)(2,1)S(1)}, bf16[2,256,384]{2,1,0:T(8,128)(2,1)S(1)}, u32[]{:S(2)}, u32[]{:S(2)}) collective-permute-start(bf16[2,256,384]{2,1,0:T(8,128)(2,1)S(1)} %pad_maximum_fusion.3), channel_id=1, source_target_pairs={{0,96},{1,97},{2,98},{3,99},{4,100},{5,101},{6,102},{7,103},{8,104... | collective-permute-start | bytes 1179656 | tf_op jit(solution)/shard_map/ppermute | solution.py:36
  165.9 2.4 %collective-permute-done.25 = bf16[256,640]{1,0:T(8,128)(2,1)S(1)} collective-permute-done((bf16[256,640]{1,0:T(8,128)(2,1)S(1)}, bf16[256,640]{1,0:T(8,128)(2,1)S(1)}, u32[]{:S(2)}, u32[]{:S(2)}) %collective-permute-start.25) | collective-permute-done | bytes 327712 | tf_op jit(solution)/shard_map/ppermute | solution.py:36
  168.5 3.7 %collective-permute-done.27 = bf16[2,256,384]{2,1,0:T(8,128)(2,1)S(1)} collective-permute-done((bf16[2,256,384]{2,1,0:T(8,128)(2,1)S(1)}, bf16[2,256,384]{2,1,0:T(8,128)(2,1)S(1)}, u32[]{:S(2)}, u32[]{:S(2)}) %collective-permute-start.27) | collective-permute-done | bytes 393248 | tf_op jit(solution)/shard_map/ppermute | solution.py:36
  178.1 2.7 %collective-permute-done.31 = bf16[256,384]{1,0:T(8,128)(2,1)S(1)} collective-permute-done((bf16[256,384]{1,0:T(8,128)(2,1)S(1)}, bf16[256,384]{1,0:T(8,128)(2,1)S(1)}, u32[]{:S(2)}, u32[]{:S(2)}) %collective-permute-start.31) | collective-permute-done | bytes 196640 | tf_op jit(solution)/shard_map/ppermute | solution.py:36
  (160 shorter events, 56.6 us)
Async XLA Ops:
  6.5 97.0 %all-gather.5.cloned.1.call-start = ((), (), s32[]{:S(2)}) async-start(), calls=%async_computation | async-start | bytes 13369344 | tf_op jit(solution)/shard_map/all_gather | solution.py:251
  7.3 142.0 %all-gather.7.cloned.1.call-start = ((), (), s32[]{:S(2)}) async-start(), calls=%async_computation.1 | async-start | bytes 3342336 | tf_op jit(solution)/shard_map/all_gather | solution.py:285
  8.3 17.1 %collective-permute-start.9 = (bf16[320,512]{1,0:T(8,128)(2,1)S(1)}, bf16[320,512]{1,0:T(8,128)(2,1)S(1)}, u32[]{:S(2)}, u32[]{:S(2)}) collective-permute-start(bf16[320,512]{1,0:T(8,128)(2,1)S(1)} %slice_bitcast_fusion.2.refs_2_), channel_id=1, source_target_pairs={{0,2},{1,3},{2,4},{3,5},{4,6},{5,7},{6,8},{7,9},{8,10},{9,11},{10,... | collective-permute-start | bytes 983048 | tf_op jit(solution)/shard_map/ppermute | solution.py:36
  10.3 15.7 %collective-permute-start.8 = (bf16[320,512]{1,0:T(8,128)(2,1)S(1)}, bf16[320,512]{1,0:T(8,128)(2,1)S(1)}, u32[]{:S(2)}, u32[]{:S(2)}) collective-permute-start(bf16[320,512]{1,0:T(8,128)(2,1)S(1)} %slice_bitcast_fusion.2.refs_2_), channel_id=1, source_target_pairs={{0,14},{1,15},{2,0},{3,1},{4,2},{5,3},{6,4},{7,5},{8,6},{9,7},{10,... | collective-permute-start | bytes 983048 | tf_op jit(solution)/shard_map/ppermute | solution.py:36
  10.4 23.4 %collective-permute-start.5 = (bf16[1,4,2,1,256,128]{5,4,2,1,3,0:T(8,128)(2,1)}, bf16[1,4,2,1,256,128]{5,4,2,1,3,0:T(8,128)(2,1)}, u32[]{:S(2)}, u32[]{:S(2)}) collective-permute-start(bf16[1,4,2,1,256,128]{5,4,2,1,3,0:T(8,128)(2,1)} %bitcast.116), channel_id=1, source_target_pairs={{0,1},{1,2},{2,3},{3,4},{4,5},{5,6},{6,7},{7,8},{8,9},{9,10},{10,1... | collective-permute-start | bytes 1572872 | tf_op jit(solution)/shard_map/ppermute | solution.py:153
  10.4 28.5 %collective-permute-start.6 = (bf16[1,4,2,1,256,128]{5,4,2,1,3,0:T(8,128)(2,1)}, bf16[1,4,2,1,256,128]{5,4,2,1,3,0:T(8,128)(2,1)}, u32[]{:S(2)}, u32[]{:S(2)}) collective-permute-start(bf16[1,4,2,1,256,128]{5,4,2,1,3,0:T(8,128)(2,1)} %bitcast.117), channel_id=1, source_target_pairs={{1,0},{2,1},{3,2},{4,3},{5,4},{6,5},{7,6},{8,7},{9,8},{10,9},{11,1... | collective-permute-start | bytes 1572872 | tf_op jit(solution)/shard_map/ppermute | solution.py:154
  13.6 15.6 %collective-permute-start = (bf16[256,1024]{1,0:T(8,128)(2,1)}, bf16[256,1024]{1,0:T(8,128)(2,1)S(1)}, u32[]{:S(2)}, u32[]{:S(2)}) collective-permute-start(bf16[256,1024]{1,0:T(8,128)(2,1)} %bitcast.1), channel_id=1, source_target_pairs={{0,16},{1,17},{2,18},{3,19},{4,20},{5,21},{6,22},{7,23},{8,24},{9,... | collective-permute-start | bytes 1572872 | tf_op jit(solution)/shard_map/ppermute | solution.py:36
  25.4 70.3 %collective-permute-start.7 = (bf16[256,1024]{1,0:T(8,128)(2,1)}, bf16[256,1024]{1,0:T(8,128)(2,1)}, u32[]{:S(2)}, u32[]{:S(2)}) collective-permute-start(bf16[256,1024]{1,0:T(8,128)(2,1)} %bitcast.1), channel_id=1, source_target_pairs={{0,128},{1,129},{2,130},{3,131},{4,132},{5,133},{6,134},{7,135},{8... | collective-permute-start | bytes 1572872 | tf_op jit(solution)/shard_map/ppermute | solution.py:36
  26.0 18.2 %collective-permute-start.11 = (bf16[320,512]{1,0:T(8,128)(2,1)S(1)}, bf16[320,512]{1,0:T(8,128)(2,1)S(1)}, u32[]{:S(2)}, u32[]{:S(2)}) collective-permute-start(bf16[320,512]{1,0:T(8,128)(2,1)S(1)} %collective-permute-done.9.refs_4_), channel_id=1, source_target_pairs={{0,2},{1,3},{2,4},{3,5},{4,6},{5,7},{6,8},{7,9},{8,10},{9,11},{10,... | collective-permute-start | bytes 983048 | tf_op jit(solution)/shard_map/ppermute | solution.py:36
  29.2 17.5 %collective-permute-start.10 = (bf16[320,512]{1,0:T(8,128)(2,1)S(1)}, bf16[320,512]{1,0:T(8,128)(2,1)S(1)}, u32[]{:S(2)}, u32[]{:S(2)}) collective-permute-start(bf16[320,512]{1,0:T(8,128)(2,1)S(1)} %collective-permute-done.8.refs_3_), channel_id=1, source_target_pairs={{0,14},{1,15},{2,0},{3,1},{4,2},{5,3},{6,4},{7,5},{8,6},{9,7},{10,... | collective-permute-start | bytes 983048 | tf_op jit(solution)/shard_map/ppermute | solution.py:36
  33.9 44.3 %collective-permute-start.1 = (bf16[2,256,1024]{2,1,0:T(8,128)(2,1)}, bf16[2,256,1024]{2,1,0:T(8,128)(2,1)}, u32[]{:S(2)}, u32[]{:S(2)}) collective-permute-start(bf16[2,256,1024]{2,1,0:T(8,128)(2,1)} %pad_maximum_fusion), channel_id=1, source_target_pairs={{0,96},{1,97},{2,98},{3,99},{4,100},{5,101},{6,102},{7,103},{8,104... | collective-permute-start | bytes 3145736 | tf_op jit(solution)/shard_map/ppermute | solution.py:36
  39.0 36.4 %collective-permute-start.2 = (bf16[2,256,1024]{2,1,0:T(8,128)(2,1)}, bf16[2,256,1024]{2,1,0:T(8,128)(2,1)}, u32[]{:S(2)}, u32[]{:S(2)}) collective-permute-start(bf16[2,256,1024]{2,1,0:T(8,128)(2,1)} %pad_maximum_fusion), channel_id=1, source_target_pairs={{0,32},{1,33},{2,34},{3,35},{4,36},{5,37},{6,38},{7,39},{8,40},{9,... | collective-permute-start | bytes 3145736 | tf_op jit(solution)/shard_map/ppermute | solution.py:36
  44.2 17.2 %collective-permute-start.13 = (bf16[320,512]{1,0:T(8,128)(2,1)S(1)}, bf16[320,512]{1,0:T(8,128)(2,1)S(1)}, u32[]{:S(2)}, u32[]{:S(2)}) collective-permute-start(bf16[320,512]{1,0:T(8,128)(2,1)S(1)} %collective-permute-done.11.refs_6_), channel_id=1, source_target_pairs={{0,2},{1,3},{2,4},{3,5},{4,6},{5,7},{6,8},{7,9},{8,10},{9,11},{10,... | collective-permute-start | bytes 983048 | tf_op jit(solution)/shard_map/ppermute | solution.py:36
  46.7 18.3 %collective-permute-start.12 = (bf16[320,512]{1,0:T(8,128)(2,1)S(1)}, bf16[320,512]{1,0:T(8,128)(2,1)S(1)}, u32[]{:S(2)}, u32[]{:S(2)}) collective-permute-start(bf16[320,512]{1,0:T(8,128)(2,1)S(1)} %collective-permute-done.10.refs_5_), channel_id=1, source_target_pairs={{0,14},{1,15},{2,0},{3,1},{4,2},{5,3},{6,4},{7,5},{8,6},{9,7},{10,... | collective-permute-start | bytes 983048 | tf_op jit(solution)/shard_map/ppermute | solution.py:36
  61.4 10.4 %collective-permute-start.14 = (bf16[160,512]{1,0:T(8,128)(2,1)S(1)}, bf16[160,512]{1,0:T(8,128)(2,1)S(1)}, u32[]{:S(2)}, u32[]{:S(2)}) collective-permute-start(bf16[160,512]{1,0:T(8,128)(2,1)S(1)} %slice.124), channel_id=1, source_target_pairs={{0,2},{1,3},{2,4},{3,5},{4,6},{5,7},{6,8},{7,9},{8,10},{9,11},{10,... | collective-permute-start | bytes 491528 | tf_op jit(solution)/shard_map/ppermute | solution.py:36
  65.0 10.3 %collective-permute-start.15 = (bf16[160,512]{1,0:T(8,128)(2,1)S(1)}, bf16[160,512]{1,0:T(8,128)(2,1)S(1)}, u32[]{:S(2)}, u32[]{:S(2)}) collective-permute-start(bf16[160,512]{1,0:T(8,128)(2,1)S(1)} %slice.125), channel_id=1, source_target_pairs={{0,14},{1,15},{2,0},{3,1},{4,2},{5,3},{6,4},{7,5},{8,6},{9,7},{10,... | collective-permute-start | bytes 491528 | tf_op jit(solution)/shard_map/ppermute | solution.py:36
  71.8 25.0 %collective-permute-start.16 = (bf16[5,320,512]{2,1,0:T(8,128)(2,1)S(1)}, bf16[5,320,512]{2,1,0:T(8,128)(2,1)S(1)}, u32[]{:S(2)}, u32[]{:S(2)}) collective-permute-start(bf16[5,320,512]{2,1,0:T(8,128)(2,1)S(1)} %bitcast_dynamic-update-slice_fusion.10), channel_id=1, source_target_pairs={{0,1},{1,0},{2,3},{3,2},{4,5},{5,4},{6,7},{7,6},{8,9},{9,8},{10,11... | collective-permute-start | bytes 4915208 | tf_op jit(solution)/shard_map/ppermute | solution.py:36
  76.5 12.2 %collective-permute-start.3 = (bf16[256,1024]{1,0:T(8,128)(2,1)S(1)}, bf16[256,1024]{1,0:T(8,128)(2,1)S(1)}, u32[]{:S(2)}, u32[]{:S(2)}) collective-permute-start(bf16[256,1024]{1,0:T(8,128)(2,1)S(1)} %slice_bitcast_fusion.1), channel_id=1, source_target_pairs={{0,32},{1,33},{2,34},{3,35},{4,36},{5,37},{6,38},{7,39},{8,40},{9,... | collective-permute-start | bytes 1572872 | tf_op jit(solution)/shard_map/ppermute | solution.py:36
  79.3 10.6 %collective-permute-start.4 = (bf16[256,1024]{1,0:T(8,128)(2,1)S(1)}, bf16[256,1024]{1,0:T(8,128)(2,1)S(1)}, u32[]{:S(2)}, u32[]{:S(2)}) collective-permute-start(bf16[256,1024]{1,0:T(8,128)(2,1)S(1)} %slice_bitcast_fusion), channel_id=1, source_target_pairs={{0,96},{1,97},{2,98},{3,99},{4,100},{5,101},{6,102},{7,103},{8,104... | collective-permute-start | bytes 1572872 | tf_op jit(solution)/shard_map/ppermute | solution.py:36
  81.1 14.6 %collective-permute-start.17 = (bf16[3,320,512]{2,1,0:T(8,128)(2,1)S(1)}, bf16[3,320,512]{2,1,0:T(8,128)(2,1)S(1)}, u32[]{:S(2)}, u32[]{:S(2)}) collective-permute-start(bf16[3,320,512]{2,1,0:T(8,128)(2,1)S(1)} %pad_maximum_fusion.1), channel_id=1, source_target_pairs={{0,1},{1,0},{2,3},{3,2},{4,5},{5,4},{6,7},{7,6},{8,9},{9,8},{10,11... | collective-permute-start | bytes 2949128 | tf_op jit(solution)/shard_map/ppermute | solution.py:36
  119.7 11.1 %collective-permute-start.22 = (bf16[2,128,640]{2,1,0:T(8,128)(2,1)S(1)}, bf16[2,128,640]{2,1,0:T(8,128)(2,1)S(1)}, u32[]{:S(2)}, u32[]{:S(2)}) collective-permute-start(bf16[2,128,640]{2,1,0:T(8,128)(2,1)S(1)} %get-tuple-element.55), channel_id=1, source_target_pairs={{0,96},{1,97},{2,98},{3,99},{4,100},{5,101},{6,102},{7,103},{8,104... | collective-permute-start | bytes 983048 | tf_op jit(solution)/shard_map/ppermute | solution.py:36
  122.8 12.6 %collective-permute-start.18 = (bf16[2,128,640]{2,1,0:T(8,128)(2,1)S(1)}, bf16[2,128,640]{2,1,0:T(8,128)(2,1)S(1)}, u32[]{:S(2)}, u32[]{:S(2)}) collective-permute-start(bf16[2,128,640]{2,1,0:T(8,128)(2,1)S(1)} %get-tuple-element.56), channel_id=1, source_target_pairs={{0,32},{1,33},{2,34},{3,35},{4,36},{5,37},{6,38},{7,39},{8,40},{9,... | collective-permute-start | bytes 983048 | tf_op jit(solution)/shard_map/ppermute | solution.py:36
  122.9 18.9 %collective-permute-start.20 = (bf16[2,128,640]{2,1,0:T(8,128)(2,1)S(1)}, bf16[2,128,640]{2,1,0:T(8,128)(2,1)}, u32[]{:S(2)}, u32[]{:S(2)}) collective-permute-start(bf16[2,128,640]{2,1,0:T(8,128)(2,1)S(1)} %slice.128), channel_id=1, source_target_pairs={{0,32},{1,33},{2,34},{3,35},{4,36},{5,37},{6,38},{7,39},{8,40},{9,... | collective-permute-start | bytes 983048 | tf_op jit(solution)/shard_map/ppermute | solution.py:36
  123.6 18.2 %collective-permute-start.21 = (bf16[2,128,640]{2,1,0:T(8,128)(2,1)S(1)}, bf16[2,128,640]{2,1,0:T(8,128)(2,1)}, u32[]{:S(2)}, u32[]{:S(2)}) collective-permute-start(bf16[2,128,640]{2,1,0:T(8,128)(2,1)S(1)} %slice.129), channel_id=1, source_target_pairs={{0,96},{1,97},{2,98},{3,99},{4,100},{5,101},{6,102},{7,103},{8,104... | collective-permute-start | bytes 983048 | tf_op jit(solution)/shard_map/ppermute | solution.py:36
  131.7 12.6 %collective-permute-start.23 = (bf16[2,128,640]{2,1,0:T(8,128)(2,1)}, bf16[2,128,640]{2,1,0:T(8,128)(2,1)}, u32[]{:S(2)}, u32[]{:S(2)}) collective-permute-start(bf16[2,128,640]{2,1,0:T(8,128)(2,1)} %add_convert_fusion.1), channel_id=1, source_target_pairs={{0,96},{1,97},{2,98},{3,99},{4,100},{5,101},{6,102},{7,103},{8,104... | collective-permute-start | bytes 983048 | tf_op jit(solution)/shard_map/ppermute | solution.py:36
  136.2 11.5 %collective-permute-start.19 = (bf16[2,128,640]{2,1,0:T(8,128)(2,1)}, bf16[2,128,640]{2,1,0:T(8,128)(2,1)}, u32[]{:S(2)}, u32[]{:S(2)}) collective-permute-start(bf16[2,128,640]{2,1,0:T(8,128)(2,1)} %add_convert_fusion.2), channel_id=1, source_target_pairs={{0,32},{1,33},{2,34},{3,35},{4,36},{5,37},{6,38},{7,39},{8,40},{9,... | collective-permute-start | bytes 983048 | tf_op jit(solution)/shard_map/ppermute | solution.py:36
  154.0 7.3 %collective-permute-start.26 = (bf16[2,128,384]{2,1,0:T(8,128)(2,1)S(1)}, bf16[2,128,384]{2,1,0:T(8,128)(2,1)S(1)}, u32[]{:S(2)}, u32[]{:S(2)}) collective-permute-start(bf16[2,128,384]{2,1,0:T(8,128)(2,1)S(1)} %get-tuple-element.61), channel_id=1, source_target_pairs={{0,32},{1,33},{2,34},{3,35},{4,36},{5,37},{6,38},{7,39},{8,40},{9,... | collective-permute-start | bytes 589832 | tf_op jit(solution)/shard_map/ppermute | solution.py:36
  154.6 7.2 %collective-permute-start.28 = (bf16[2,128,384]{2,1,0:T(8,128)(2,1)S(1)}, bf16[2,128,384]{2,1,0:T(8,128)(2,1)S(1)}, u32[]{:S(2)}, u32[]{:S(2)}) collective-permute-start(bf16[2,128,384]{2,1,0:T(8,128)(2,1)S(1)} %get-tuple-element.62), channel_id=1, source_target_pairs={{0,96},{1,97},{2,98},{3,99},{4,100},{5,101},{6,102},{7,103},{8,104... | collective-permute-start | bytes 589832 | tf_op jit(solution)/shard_map/ppermute | solution.py:36
  157.5 8.4 %collective-permute-start.24 = (bf16[256,640]{1,0:T(8,128)(2,1)S(1)}, bf16[256,640]{1,0:T(8,128)(2,1)S(1)}, u32[]{:S(2)}, u32[]{:S(2)}) collective-permute-start(bf16[256,640]{1,0:T(8,128)(2,1)S(1)} %get-tuple-element.53), channel_id=1, source_target_pairs={{0,128},{1,129},{2,130},{3,131},{4,132},{5,133},{6,134},{7,135},{8... | collective-permute-start | bytes 983048 | tf_op jit(solution)/shard_map/ppermute | solution.py:36
  159.1 9.2 %collective-permute-start.25 = (bf16[256,640]{1,0:T(8,128)(2,1)S(1)}, bf16[256,640]{1,0:T(8,128)(2,1)S(1)}, u32[]{:S(2)}, u32[]{:S(2)}) collective-permute-start(bf16[256,640]{1,0:T(8,128)(2,1)S(1)} %get-tuple-element.54), channel_id=1, source_target_pairs={{0,144},{1,145},{2,146},{3,147},{4,148},{5,149},{6,150},{7,151},{8... | collective-permute-start | bytes 983048 | tf_op jit(solution)/shard_map/ppermute | solution.py:36
  161.5 10.6 %collective-permute-start.27 = (bf16[2,256,384]{2,1,0:T(8,128)(2,1)S(1)}, bf16[2,256,384]{2,1,0:T(8,128)(2,1)S(1)}, u32[]{:S(2)}, u32[]{:S(2)}) collective-permute-start(bf16[2,256,384]{2,1,0:T(8,128)(2,1)S(1)} %pad_maximum_fusion.2), channel_id=1, source_target_pairs={{0,32},{1,33},{2,34},{3,35},{4,36},{5,37},{6,38},{7,39},{8,40},{9,... | collective-permute-start | bytes 1179656 | tf_op jit(solution)/shard_map/ppermute | solution.py:36
  161.9 10.2 %collective-permute-start.29 = (bf16[2,256,384]{2,1,0:T(8,128)(2,1)S(1)}, bf16[2,256,384]{2,1,0:T(8,128)(2,1)S(1)}, u32[]{:S(2)}, u32[]{:S(2)}) collective-permute-start(bf16[2,256,384]{2,1,0:T(8,128)(2,1)S(1)} %pad_maximum_fusion.3), channel_id=1, source_target_pairs={{0,96},{1,97},{2,98},{3,99},{4,100},{5,101},{6,102},{7,103},{8,104... | collective-permute-start | bytes 1179656 | tf_op jit(solution)/shard_map/ppermute | solution.py:36
  (26 other events, 314.6 us)
Sparse Core Ops, SparseCore 0:
  9.2 94.2 all-gather.4
  105.3 42.9 all-gather.6
